TPU v7x, 256 devices: a whole 4x4x8 slice. The times are simulated.
256 devices in a mesh: wave: 64 (over x, z, core), lev: 4 (over y).
Axes of the slice: x: 4, y: 4, z: 8, core: 2. Of those that a mesh axis runs over, the one named last changes fastest.
Arguments:
- spectral: bfloat16 [1280, 3, 2, 24, 1280], P('wave', None, None, 'lev'), may hold values from -0.119628906 to 0.119628906
- legendre: bfloat16 [1280, 1280, 512], P(('wave', 'lev')), may hold values from -0.15625 to 0.15625
- wave_map: int32 [1280], replicated, may hold values from 0 to 1279, each once
- row_map: int32 [512], replicated, may hold values from 0 to 511, each once
- points: int32 [512], replicated, may hold values from 20 to 5136, as said below
- row_weight: float32 [512], replicated, may hold values from 40 to 400
- thickness: float32 [24], replicated, may hold values from 0.3 to 3
Outputs:
- spec_tend: bfloat16 [1280, 3, 2, 24, 1280], P('wave', None, None, 'lev')
- grid_tend: bfloat16 [512, 24, 5376], P(('wave', 'lev'))
Inputs may be any that keep to these rules, and one draw needn't show every extreme that they name: `wave_map`: each slot holds a different wavenumber. `row_map`: each latitude row is held by one slot. The rows are distinct rows of an octahedral grid of 2560 rows; a row j rows from the nearer pole (j from 0) has 20 + 4 j points; one row lies next to the equator.
All inputs are finite; a program needn't handle non-finite values.
Results may differ from a plain program's by a relative error of at most 0.009.
Values may be sent and summed in bfloat16 or wider, within the bound.
A program may use at most 64 MiB of HBM per device.

v0:
```python
import jax
import jax.numpy as jnp
from jax import lax
from jax.sharding import PartitionSpec as P

PBUF = 5376


adiabatic_exponent = 2.0 / 7.0
block_width = 768


def tendencies(quantity_pile, thickness):
    vorticity = quantity_pile[0]
    flow_spreading_grid = quantity_pile[1]
    thermal_state_grid = quantity_pile[2]
    upward_motion = -jnp.cumsum(thickness[:, None] * flow_spreading_grid, axis=0)
    ground_barometric_load = jnp.cumsum(thickness) - 0.5 * thickness
    rotation_rate_change = -vorticity * flow_spreading_grid
    spreading_rate_change = 0.5 * (
        vorticity * vorticity - flow_spreading_grid * flow_spreading_grid
    )
    warming_rate = (
        -thermal_state_grid * flow_spreading_grid
        + adiabatic_exponent * thermal_state_grid * upward_motion / ground_barometric_load[:, None]
    )
    return jnp.stack([rotation_rate_change, spreading_rate_change, warming_rate]).astype(
        jnp.bfloat16
    )


def row_trip(fourier_row, slot_waves, row_points, row_scale, thickness):
    levels = thickness.shape[0]
    waves_all = slot_waves.shape[0]
    weights = jnp.where(slot_waves == 0, 1.0, 2.0).astype(jnp.float32)
    lifted = (fourier_row.astype(jnp.float32) * weights[:, None, None, None]).astype(jnp.bfloat16)
    left_side = lifted.transpose(1, 3, 2, 0).reshape(3 * levels, 2 * waves_all)
    points_float = row_points.astype(jnp.float32)
    base_ids = jnp.arange(block_width, dtype=jnp.int32)
    base_res = slot_waves[:, None] * base_ids[None, :] % row_points
    base_angle = 2.0 * jnp.pi * base_res.astype(jnp.float32) / points_float
    base_cos = jnp.cos(base_angle)
    base_sin = jnp.sin(base_angle)
    step_res = slot_waves * block_width % row_points
    wave_ok = (2 * slot_waves < row_points)[:, None]

    def one_block(block, carry):
        running, pieces = carry
        first_point = block * block_width
        phase = 2.0 * jnp.pi * (step_res * block % row_points).astype(jnp.float32) / points_float
        phase_cos = jnp.cos(phase)[:, None]
        phase_sin = jnp.sin(phase)[:, None]
        block_cos = base_cos * phase_cos - base_sin * phase_sin
        block_sin = base_sin * phase_cos + base_cos * phase_sin
        active = wave_ok & ((first_point + base_ids)[None, :] < row_points)
        tables = jnp.concatenate(
            [
                jnp.where(active, block_cos, 0.0).astype(jnp.bfloat16),
                jnp.where(active, -block_sin, 0.0).astype(jnp.bfloat16),
            ],
            axis=0,
        )
        quantity_pile = jnp.dot(left_side, tables, preferred_element_type=jnp.float32)
        tendency = tendencies(quantity_pile.reshape(3, levels, block_width), thickness)
        added = lax.dot_general(
            tendency.reshape(3 * levels, block_width),
            tables,
            (((1,), (1,)), ((), ())),
            preferred_element_type=jnp.float32,
        )
        pieces = lax.dynamic_update_slice(pieces, tendency[2], (jnp.int32(0), first_point))
        return (running + added, pieces)

    block_count = (row_points + block_width - 1) // block_width
    start = (
        jnp.zeros((3 * levels, 2 * waves_all), jnp.float32),
        jnp.zeros((levels, PBUF), jnp.bfloat16),
    )
    running, pieces = lax.fori_loop(jnp.int32(0), block_count, one_block, start)
    back_row = (
        (running * row_scale)
        .astype(jnp.bfloat16)
        .reshape(3, levels, 2, waves_all)
        .transpose(3, 0, 2, 1)
    )
    return (back_row, pieces)


def on_device(spectral, legendre, wave_map, row_map, points, row_weight, thickness):
    wave_count = lax.axis_size("wave")
    level_count = lax.axis_size("lev")
    device_count = wave_count * level_count
    device_flat = lax.axis_index("wave") * level_count + lax.axis_index("lev")
    slots_here = legendre.shape[0]
    waves_all = wave_map.shape[0]
    rows_all = row_map.shape[0]
    rows_here = rows_all // device_count
    levels = thickness.shape[0]
    columns = 6 * levels
    slot_coefs = lax.all_to_all(spectral, "lev", split_axis=0, concat_axis=3, tiled=True)
    local_waves = lax.dynamic_slice_in_dim(wave_map, device_flat * slots_here, slots_here)
    kept_mask = jnp.arange(waves_all, dtype=jnp.int32)[None, :] < (waves_all - local_waves)[:, None]
    masked_coefs = jnp.where(
        kept_mask[:, None, None, None, :], slot_coefs, jnp.zeros((), jnp.bfloat16)
    )
    fourier = jnp.einsum(
        "sfplk,skr->sfplr", masked_coefs, legendre, preferred_element_type=jnp.float32
    ).astype(jnp.bfloat16)
    fourier = fourier.reshape(slots_here, columns, rows_all)
    outgoing = jnp.take(fourier, row_map, axis=2)
    arrived = lax.all_to_all(
        lax.all_to_all(outgoing, "wave", split_axis=2, concat_axis=0, tiled=True),
        "lev",
        split_axis=2,
        concat_axis=0,
        tiled=True,
    )
    arrival_waves = (
        wave_map.reshape(wave_count, level_count, slots_here).transpose(1, 0, 2).reshape(-1)
    )
    owned_rows = lax.dynamic_slice_in_dim(row_map, device_flat * rows_here, rows_here)
    owned_points = jnp.take(points, owned_rows)
    owned_scales = jnp.take(row_weight, owned_rows) / owned_points.astype(jnp.float32)
    by_row = arrived.reshape(waves_all, 3, 2, levels, rows_here).transpose(4, 0, 1, 2, 3)

    def one_row(bundle):
        fourier_row, row_points, row_scale = bundle
        return row_trip(fourier_row, arrival_waves, row_points, row_scale, thickness)

    row_backs, row_temps = lax.map(one_row, (by_row, owned_points, owned_scales))
    returning = row_backs.transpose(1, 2, 3, 4, 0).reshape(waves_all, columns, rows_here)
    partial_back = lax.all_to_all(returning, "lev", split_axis=0, concat_axis=2, tiled=True)
    gathered = lax.all_to_all(partial_back, "wave", split_axis=0, concat_axis=2, tiled=True)
    positions = (
        jnp.zeros((rows_all,), jnp.int32).at[row_map].set(jnp.arange(rows_all, dtype=jnp.int32))
    )
    by_latitude = jnp.take(gathered, positions, axis=2)
    direct_sums = jnp.einsum(
        "scr,skr->sck", by_latitude, legendre, preferred_element_type=jnp.float32
    )
    spec_local = (
        jnp.where(kept_mask[:, None, :], direct_sums, 0.0)
        .astype(jnp.bfloat16)
        .reshape(slots_here, 3, 2, levels, waves_all)
    )
    spec_tend = lax.all_to_all(spec_local, "lev", split_axis=3, concat_axis=0, tiled=True)
    return (spec_tend, row_temps)


def solution(mesh):
    return jax.shard_map(
        on_device,
        mesh=mesh,
        in_specs=(
            P("wave", None, None, "lev", None),
            P(("wave", "lev"), None, None),
            P(),
            P(),
            P(),
            P(),
            P(),
        ),
        out_specs=(P("wave", None, None, "lev", None), P(("wave", "lev"), None, None)),
        check_vma=False,
    )
```

profile of v0, /device:TPU:1, one launch (start us, length us, event | category | flops | bytes accessed | tf_op | source)
XLA Modules:
  0.0 1119.6 jit_solution(1088966744466054127)
XLA Ops:
  6.0 21.7 %all-to-all-done = bf16[20,3,2,6,1280]{4,2,3,1,0:T(2,128)(2,1)S(1)} async-done(((bf16[20,3,2,6,1280]{4,2,3,1,0:T(2,128)(2,1)}), bf16[20,3,2,6,1280]{4,2,3,1,0:T(2,128)(2,1)S(1)}, u32[]{:S(2)}, u32[]{:S(2)}) %all-to-all-start) | async-done | bytes 1843232 | tf_op jit(solution)/shard_map/all_to_all | solution.py:100
  42.5 14.2 %all-to-all-start.1 = ((bf16[64,2,2880]{2,1,0:T(2,128)(2,1)}), bf16[64,2,2880]{2,1,0:T(2,128)(2,1)S(1)}, u32[]{:S(2)}, u32[]{:S(2)}) async-start(bf16[64,2,2880]{2,1,0:T(2,128)(2,1)} %reshape.236), calls=%async_computation.1 | async-start | bytes 1507328 | tf_op jit(solution)/shard_map/all_to_all | solution.py:112
  58.0 20.9 %all-to-all-done.1 = bf16[64,2,2880]{2,1,0:T(2,128)(2,1)S(1)} async-done(((bf16[64,2,2880]{2,1,0:T(2,128)(2,1)}), bf16[64,2,2880]{2,1,0:T(2,128)(2,1)S(1)}, u32[]{:S(2)}, u32[]{:S(2)}) %all-to-all-start.1) | async-done | bytes 737312 | tf_op jit(solution)/shard_map/all_to_all | solution.py:112
  90.8 9.5 all-to-all-done.2
  102.3 848.2 %while.61 = (s32[]{:T(128)}, bf16[2,1280,3,2,24]{1,4,3,2,0:T(8,128)(2,1)}, bf16[2,24,5376]{2,1,0:T(8,128)(2,1)}, s32[2]{0:T(128)}, s32[1280]{0:T(1024)S(1)}, /*i...) while((s32[]{:T(128)}, ...), condition=%wide.wide.region_5.7_spmd, body=%wide.wide.region_1.0_spmd.sunk | while | flops 606554432 | bytes 36326776 | solution.py:130
  109.7 444.7 %while.62 = (s32[]{:T(128)}, f32[72,2560]{1,0:T(8,128)S(1)}, bf16[24,5376]{1,0:T(8,128)(2,1)S(1)}, s32[]{:T(128)}, pred[1280,1]{0,1:T(4,128)(4,1)}, /*index=5*/s...) while((s32[]{:T(128)}, f32[72,2560]{1,0:T(8,128)S(1)}, ...), condition=%wide.region_4.5_spmd.clone.clone, body=%wide.region_2.4_spmd.clone.clone.sunk | while | flops 605617472 | bytes 25817560 | solution.py:79
  112.0 56.0 %fusion.59 = (bf16[1280,768]{1,0:T(8,128)(2,1)S(1)}, bf16[1280,768]{1,0:T(8,128)(2,1)S(1)}) fusion(f32[1280]{0:T(1024)S(1)} %get-tuple-element.871, f32[1280]{0:T(1024)S(1)} %get-tuple-element.872, f32[]{:T(128)} %get-tuple-element.927, pred[]{:T(512)} %get-tuple-element.926, s32[]{:T(128)} %get-tuple-element.925, s32[1280]{0:T(1024)} %get-tuple-element.931, ...), kind=kLoop, calls=%fused_computation.11.clone.1 | loop fusion | flops 22609920 | bytes 3949577 | tf_op jit(solution)/shard_map/while/body/eval_jaxpr/while/body/convert_element_type | solution.py:58
  175.5 56.0 %fusion.59 = (bf16[1280,768]{1,0:T(8,128)(2,1)S(1)}, bf16[1280,768]{1,0:T(8,128)(2,1)S(1)}) fusion(f32[1280]{0:T(1024)S(1)} %get-tuple-element.871, f32[1280]{0:T(1024)S(1)} %get-tuple-element.872, f32[]{:T(128)} %get-tuple-element.927, pred[]{:T(512)} %get-tuple-element.926, s32[]{:T(128)} %get-tuple-element.925, s32[1280]{0:T(1024)} %get-tuple-element.931, ...), kind=kLoop, calls=%fused_computation.11.clone.1 | loop fusion | flops 22609920 | bytes 3949577 | tf_op jit(solution)/shard_map/while/body/eval_jaxpr/while/body/convert_element_type | solution.py:58
  239.0 56.0 %fusion.59 = (bf16[1280,768]{1,0:T(8,128)(2,1)S(1)}, bf16[1280,768]{1,0:T(8,128)(2,1)S(1)}) fusion(f32[1280]{0:T(1024)S(1)} %get-tuple-element.871, f32[1280]{0:T(1024)S(1)} %get-tuple-element.872, f32[]{:T(128)} %get-tuple-element.927, pred[]{:T(512)} %get-tuple-element.926, s32[]{:T(128)} %get-tuple-element.925, s32[1280]{0:T(1024)} %get-tuple-element.931, ...), kind=kLoop, calls=%fused_computation.11.clone.1 | loop fusion | flops 22609920 | bytes 3949577 | tf_op jit(solution)/shard_map/while/body/eval_jaxpr/while/body/convert_element_type | solution.py:58
  302.6 56.0 %fusion.59 = (bf16[1280,768]{1,0:T(8,128)(2,1)S(1)}, bf16[1280,768]{1,0:T(8,128)(2,1)S(1)}) fusion(f32[1280]{0:T(1024)S(1)} %get-tuple-element.871, f32[1280]{0:T(1024)S(1)} %get-tuple-element.872, f32[]{:T(128)} %get-tuple-element.927, pred[]{:T(512)} %get-tuple-element.926, s32[]{:T(128)} %get-tuple-element.925, s32[1280]{0:T(1024)} %get-tuple-element.931, ...), kind=kLoop, calls=%fused_computation.11.clone.1 | loop fusion | flops 22609920 | bytes 3949577 | tf_op jit(solution)/shard_map/while/body/eval_jaxpr/while/body/convert_element_type | solution.py:58
  366.1 56.0 %fusion.59 = (bf16[1280,768]{1,0:T(8,128)(2,1)S(1)}, bf16[1280,768]{1,0:T(8,128)(2,1)S(1)}) fusion(f32[1280]{0:T(1024)S(1)} %get-tuple-element.871, f32[1280]{0:T(1024)S(1)} %get-tuple-element.872, f32[]{:T(128)} %get-tuple-element.927, pred[]{:T(512)} %get-tuple-element.926, s32[]{:T(128)} %get-tuple-element.925, s32[1280]{0:T(1024)} %get-tuple-element.931, ...), kind=kLoop, calls=%fused_computation.11.clone.1 | loop fusion | flops 22609920 | bytes 3949577 | tf_op jit(solution)/shard_map/while/body/eval_jaxpr/while/body/convert_element_type | solution.py:58
  429.6 56.0 %fusion.59 = (bf16[1280,768]{1,0:T(8,128)(2,1)S(1)}, bf16[1280,768]{1,0:T(8,128)(2,1)S(1)}) fusion(f32[1280]{0:T(1024)S(1)} %get-tuple-element.871, f32[1280]{0:T(1024)S(1)} %get-tuple-element.872, f32[]{:T(128)} %get-tuple-element.927, pred[]{:T(512)} %get-tuple-element.926, s32[]{:T(128)} %get-tuple-element.925, s32[1280]{0:T(1024)} %get-tuple-element.931, ...), kind=kLoop, calls=%fused_computation.11.clone.1 | loop fusion | flops 22609920 | bytes 3949577 | tf_op jit(solution)/shard_map/while/body/eval_jaxpr/while/body/convert_element_type | solution.py:58
  493.2 56.0 %fusion.59 = (bf16[1280,768]{1,0:T(8,128)(2,1)S(1)}, bf16[1280,768]{1,0:T(8,128)(2,1)S(1)}) fusion(f32[1280]{0:T(1024)S(1)} %get-tuple-element.871, f32[1280]{0:T(1024)S(1)} %get-tuple-element.872, f32[]{:T(128)} %get-tuple-element.927, pred[]{:T(512)} %get-tuple-element.926, s32[]{:T(128)} %get-tuple-element.925, s32[1280]{0:T(1024)} %get-tuple-element.931, ...), kind=kLoop, calls=%fused_computation.11.clone.1 | loop fusion | flops 22609920 | bytes 3949577 | tf_op jit(solution)/shard_map/while/body/eval_jaxpr/while/body/convert_element_type | solution.py:58
  565.5 381.2 %while.62 = (s32[]{:T(128)}, f32[72,2560]{1,0:T(8,128)S(1)}, bf16[24,5376]{1,0:T(8,128)(2,1)S(1)}, s32[]{:T(128)}, pred[1280,1]{0,1:T(4,128)(4,1)}, /*index=5*/s...) while((s32[]{:T(128)}, f32[72,2560]{1,0:T(8,128)S(1)}, ...), condition=%wide.region_4.5_spmd.clone.clone, body=%wide.region_2.4_spmd.clone.clone.sunk | while | flops 605617472 | bytes 25817560 | solution.py:79
  567.8 56.0 %fusion.59 = (bf16[1280,768]{1,0:T(8,128)(2,1)S(1)}, bf16[1280,768]{1,0:T(8,128)(2,1)S(1)}) fusion(f32[1280]{0:T(1024)S(1)} %get-tuple-element.871, f32[1280]{0:T(1024)S(1)} %get-tuple-element.872, f32[]{:T(128)} %get-tuple-element.927, pred[]{:T(512)} %get-tuple-element.926, s32[]{:T(128)} %get-tuple-element.925, s32[1280]{0:T(1024)} %get-tuple-element.931, ...), kind=kLoop, calls=%fused_computation.11.clone.1 | loop fusion | flops 22609920 | bytes 3949577 | tf_op jit(solution)/shard_map/while/body/eval_jaxpr/while/body/convert_element_type | solution.py:58
  631.4 56.0 %fusion.59 = (bf16[1280,768]{1,0:T(8,128)(2,1)S(1)}, bf16[1280,768]{1,0:T(8,128)(2,1)S(1)}) fusion(f32[1280]{0:T(1024)S(1)} %get-tuple-element.871, f32[1280]{0:T(1024)S(1)} %get-tuple-element.872, f32[]{:T(128)} %get-tuple-element.927, pred[]{:T(512)} %get-tuple-element.926, s32[]{:T(128)} %get-tuple-element.925, s32[1280]{0:T(1024)} %get-tuple-element.931, ...), kind=kLoop, calls=%fused_computation.11.clone.1 | loop fusion | flops 22609920 | bytes 3949577 | tf_op jit(solution)/shard_map/while/body/eval_jaxpr/while/body/convert_element_type | solution.py:58
  694.9 56.0 %fusion.59 = (bf16[1280,768]{1,0:T(8,128)(2,1)S(1)}, bf16[1280,768]{1,0:T(8,128)(2,1)S(1)}) fusion(f32[1280]{0:T(1024)S(1)} %get-tuple-element.871, f32[1280]{0:T(1024)S(1)} %get-tuple-element.872, f32[]{:T(128)} %get-tuple-element.927, pred[]{:T(512)} %get-tuple-element.926, s32[]{:T(128)} %get-tuple-element.925, s32[1280]{0:T(1024)} %get-tuple-element.931, ...), kind=kLoop, calls=%fused_computation.11.clone.1 | loop fusion | flops 22609920 | bytes 3949577 | tf_op jit(solution)/shard_map/while/body/eval_jaxpr/while/body/convert_element_type | solution.py:58
  758.4 56.0 %fusion.59 = (bf16[1280,768]{1,0:T(8,128)(2,1)S(1)}, bf16[1280,768]{1,0:T(8,128)(2,1)S(1)}) fusion(f32[1280]{0:T(1024)S(1)} %get-tuple-element.871, f32[1280]{0:T(1024)S(1)} %get-tuple-element.872, f32[]{:T(128)} %get-tuple-element.927, pred[]{:T(512)} %get-tuple-element.926, s32[]{:T(128)} %get-tuple-element.925, s32[1280]{0:T(1024)} %get-tuple-element.931, ...), kind=kLoop, calls=%fused_computation.11.clone.1 | loop fusion | flops 22609920 | bytes 3949577 | tf_op jit(solution)/shard_map/while/body/eval_jaxpr/while/body/convert_element_type | solution.py:58
  822.0 56.0 %fusion.59 = (bf16[1280,768]{1,0:T(8,128)(2,1)S(1)}, bf16[1280,768]{1,0:T(8,128)(2,1)S(1)}) fusion(f32[1280]{0:T(1024)S(1)} %get-tuple-element.871, f32[1280]{0:T(1024)S(1)} %get-tuple-element.872, f32[]{:T(128)} %get-tuple-element.927, pred[]{:T(512)} %get-tuple-element.926, s32[]{:T(128)} %get-tuple-element.925, s32[1280]{0:T(1024)} %get-tuple-element.931, ...), kind=kLoop, calls=%fused_computation.11.clone.1 | loop fusion | flops 22609920 | bytes 3949577 | tf_op jit(solution)/shard_map/while/body/eval_jaxpr/while/body/convert_element_type | solution.py:58
  885.5 56.0 %fusion.59 = (bf16[1280,768]{1,0:T(8,128)(2,1)S(1)}, bf16[1280,768]{1,0:T(8,128)(2,1)S(1)}) fusion(f32[1280]{0:T(1024)S(1)} %get-tuple-element.871, f32[1280]{0:T(1024)S(1)} %get-tuple-element.872, f32[]{:T(128)} %get-tuple-element.927, pred[]{:T(512)} %get-tuple-element.926, s32[]{:T(128)} %get-tuple-element.925, s32[1280]{0:T(1024)} %get-tuple-element.931, ...), kind=kLoop, calls=%fused_computation.11.clone.1 | loop fusion | flops 22609920 | bytes 3949577 | tf_op jit(solution)/shard_map/while/body/eval_jaxpr/while/body/convert_element_type | solution.py:58
  953.7 13.6 %all_to_all.105 = bf16[1280,144,2]{1,2,0:T(2,128)(2,1)S(1)} all-to-all(bf16[1280,144,2]{1,2,0:T(2,128)(2,1)S(1)} %copy.85), channel_id=1, replica_groups=mesh['wave'=64,'lev'=4] {'lev'}, dimensions={0} | all-to-all | bytes 1474560 | tf_op jit(solution)/shard_map/all_to_all | solution.py:132
  972.4 70.8 %all-to-all-start.4 = ((bf16[320,144,8]{1,2,0:T(8,128)(2,1)}), bf16[320,144,8]{1,2,0:T(8,128)(2,1)S(1)}, u32[]{:S(2)}, u32[]{:S(2)}) async-start(bf16[320,144,8]{1,2,0:T(8,128)(2,1)} %copy.88), calls=%async_computation.4 | async-start | bytes 2621440 | tf_op jit(solution)/shard_map/all_to_all | solution.py:133
  1045.9 31.5 %all-to-all-done.4 = bf16[320,144,8]{1,2,0:T(8,128)(2,1)S(1)} async-done(((bf16[320,144,8]{1,2,0:T(8,128)(2,1)}), bf16[320,144,8]{1,2,0:T(8,128)(2,1)S(1)}, u32[]{:S(2)}, u32[]{:S(2)}) %all-to-all-start.4) | async-done | bytes 737312 | tf_op jit(solution)/shard_map/all_to_all | solution.py:133
  1090.8 26.3 %all_to_all.106 = bf16[5,3,2,24,1280]{4,2,1,0,3:T(2,128)(2,1)S(1)} all-to-all(bf16[5,3,2,24,1280]{4,2,1,0,3:T(2,128)(2,1)S(1)} %copy.92), channel_id=1, replica_groups=mesh['wave'=64,'lev'=4] {'lev'}, dimensions={3} | all-to-all | bytes 3686400 | tf_op jit(solution)/shard_map/all_to_all | solution.py:146
  (363 shorter events, 175.2 us)
Async XLA Ops:
  0.6 86.8 %copy-start = (s32[512]{0:T(512)S(1)}, s32[512]{0:T(512)}, u32[]{:S(2)}) copy-start(s32[512]{0:T(512)} %param.17) | copy-start | bytes 6148
  0.7 27.0 %all-to-all-start = ((bf16[20,3,2,6,1280]{4,2,3,1,0:T(2,128)(2,1)}), bf16[20,3,2,6,1280]{4,2,3,1,0:T(2,128)(2,1)S(1)}, u32[]{:S(2)}, u32[]{:S(2)}) async-start(bf16[20,3,2,6,1280]{4,2,3,1,0:T(2,128)(2,1)} %param.13), calls=%async_computation | async-start | bytes 3686400 | tf_op jit(solution)/shard_map/all_to_all | solution.py:100
  5.9 24.5 %copy-start.15 = (s32[512]{0:T(512)}, s32[512]{0:T(512)S(1)}, u32[]{:S(2)}) copy-start(s32[512]{0:T(512)S(1)} %compare_select_fusion.2) | copy-start | bytes 6148
  6.0 24.4 %copy-start.11 = (pred[5,1280]{1,0:T(8,128)(4,1)}, pred[5,1280]{1,0:T(8,128)(4,1)S(1)}, u32[]{:S(2)}) copy-start(pred[5,1280]{1,0:T(8,128)(4,1)S(1)} %iota_compare_fusion) | copy-start | bytes 19204
  42.5 36.5 %all-to-all-start.1 = ((bf16[64,2,2880]{2,1,0:T(2,128)(2,1)}), bf16[64,2,2880]{2,1,0:T(2,128)(2,1)S(1)}, u32[]{:S(2)}, u32[]{:S(2)}) async-start(bf16[64,2,2880]{2,1,0:T(2,128)(2,1)} %reshape.236), calls=%async_computation.1 | async-start | bytes 1507328 | tf_op jit(solution)/shard_map/all_to_all | solution.py:112
  56.9 24.7 %copy-start.8 = (s32[4,64,5]{2,1,0:T(8,128)}, s32[4,64,5]{2,1,0:T(8,128)S(1)}, u32[]{:S(2)}) copy-start(s32[4,64,5]{2,1,0:T(8,128)S(1)} %copy.72) | copy-start | bytes 15364
  82.1 6.6 copy-start.9
  83.7 16.5 %all-to-all-start.2 = ((bf16[320,144,8]{0,1,2:T(8,128)(2,1)}), bf16[320,144,8]{0,1,2:T(8,128)(2,1)S(1)}, u32[]{:S(2)}, u32[]{:S(2)}) async-start(bf16[320,144,8]{0,1,2:T(8,128)(2,1)} %copy.78), calls=%async_computation.2 | async-start | bytes 1769472 | tf_op jit(solution)/shard_map/all_to_all | solution.py:111
  102.3 7.4 copy-start.6
  109.7 59.1 %copy-start.4 = (bf16[72,2560]{1,0:T(8,128)(2,1)}, bf16[72,2560]{1,0:T(8,128)(2,1)S(1)}, u32[]{:S(2)}) copy-start(bf16[72,2560]{1,0:T(8,128)(2,1)S(1)} %get-tuple-element.928) | copy-start | bytes 1105924 | tf_op jit(solution)/shard_map/while/body/eval_jaxpr/while
  173.2 59.1 %copy-start.4 = (bf16[72,2560]{1,0:T(8,128)(2,1)}, bf16[72,2560]{1,0:T(8,128)(2,1)S(1)}, u32[]{:S(2)}) copy-start(bf16[72,2560]{1,0:T(8,128)(2,1)S(1)} %get-tuple-element.928) | copy-start | bytes 1105924 | tf_op jit(solution)/shard_map/while/body/eval_jaxpr/while
  236.7 59.1 %copy-start.4 = (bf16[72,2560]{1,0:T(8,128)(2,1)}, bf16[72,2560]{1,0:T(8,128)(2,1)S(1)}, u32[]{:S(2)}) copy-start(bf16[72,2560]{1,0:T(8,128)(2,1)S(1)} %get-tuple-element.928) | copy-start | bytes 1105924 | tf_op jit(solution)/shard_map/while/body/eval_jaxpr/while
  300.3 59.1 %copy-start.4 = (bf16[72,2560]{1,0:T(8,128)(2,1)}, bf16[72,2560]{1,0:T(8,128)(2,1)S(1)}, u32[]{:S(2)}) copy-start(bf16[72,2560]{1,0:T(8,128)(2,1)S(1)} %get-tuple-element.928) | copy-start | bytes 1105924 | tf_op jit(solution)/shard_map/while/body/eval_jaxpr/while
  363.8 59.1 %copy-start.4 = (bf16[72,2560]{1,0:T(8,128)(2,1)}, bf16[72,2560]{1,0:T(8,128)(2,1)S(1)}, u32[]{:S(2)}) copy-start(bf16[72,2560]{1,0:T(8,128)(2,1)S(1)} %get-tuple-element.928) | copy-start | bytes 1105924 | tf_op jit(solution)/shard_map/while/body/eval_jaxpr/while
  427.3 59.1 %copy-start.4 = (bf16[72,2560]{1,0:T(8,128)(2,1)}, bf16[72,2560]{1,0:T(8,128)(2,1)S(1)}, u32[]{:S(2)}) copy-start(bf16[72,2560]{1,0:T(8,128)(2,1)S(1)} %get-tuple-element.928) | copy-start | bytes 1105924 | tf_op jit(solution)/shard_map/while/body/eval_jaxpr/while
  490.9 59.1 %copy-start.4 = (bf16[72,2560]{1,0:T(8,128)(2,1)}, bf16[72,2560]{1,0:T(8,128)(2,1)S(1)}, u32[]{:S(2)}) copy-start(bf16[72,2560]{1,0:T(8,128)(2,1)S(1)} %get-tuple-element.928) | copy-start | bytes 1105924 | tf_op jit(solution)/shard_map/while/body/eval_jaxpr/while
  558.1 7.4 copy-start.6
  565.5 59.1 %copy-start.4 = (bf16[72,2560]{1,0:T(8,128)(2,1)}, bf16[72,2560]{1,0:T(8,128)(2,1)S(1)}, u32[]{:S(2)}) copy-start(bf16[72,2560]{1,0:T(8,128)(2,1)S(1)} %get-tuple-element.928) | copy-start | bytes 1105924 | tf_op jit(solution)/shard_map/while/body/eval_jaxpr/while
  629.0 59.1 %copy-start.4 = (bf16[72,2560]{1,0:T(8,128)(2,1)}, bf16[72,2560]{1,0:T(8,128)(2,1)S(1)}, u32[]{:S(2)}) copy-start(bf16[72,2560]{1,0:T(8,128)(2,1)S(1)} %get-tuple-element.928) | copy-start | bytes 1105924 | tf_op jit(solution)/shard_map/while/body/eval_jaxpr/while
  692.6 59.1 %copy-start.4 = (bf16[72,2560]{1,0:T(8,128)(2,1)}, bf16[72,2560]{1,0:T(8,128)(2,1)S(1)}, u32[]{:S(2)}) copy-start(bf16[72,2560]{1,0:T(8,128)(2,1)S(1)} %get-tuple-element.928) | copy-start | bytes 1105924 | tf_op jit(solution)/shard_map/while/body/eval_jaxpr/while
  756.1 59.1 %copy-start.4 = (bf16[72,2560]{1,0:T(8,128)(2,1)}, bf16[72,2560]{1,0:T(8,128)(2,1)S(1)}, u32[]{:S(2)}) copy-start(bf16[72,2560]{1,0:T(8,128)(2,1)S(1)} %get-tuple-element.928) | copy-start | bytes 1105924 | tf_op jit(solution)/shard_map/while/body/eval_jaxpr/while
  819.6 59.1 %copy-start.4 = (bf16[72,2560]{1,0:T(8,128)(2,1)}, bf16[72,2560]{1,0:T(8,128)(2,1)S(1)}, u32[]{:S(2)}) copy-start(bf16[72,2560]{1,0:T(8,128)(2,1)S(1)} %get-tuple-element.928) | copy-start | bytes 1105924 | tf_op jit(solution)/shard_map/while/body/eval_jaxpr/while
  883.2 59.1 %copy-start.4 = (bf16[72,2560]{1,0:T(8,128)(2,1)}, bf16[72,2560]{1,0:T(8,128)(2,1)S(1)}, u32[]{:S(2)}) copy-start(bf16[72,2560]{1,0:T(8,128)(2,1)S(1)} %get-tuple-element.928) | copy-start | bytes 1105924 | tf_op jit(solution)/shard_map/while/body/eval_jaxpr/while
  972.4 105.0 %all-to-all-start.4 = ((bf16[320,144,8]{1,2,0:T(8,128)(2,1)}), bf16[320,144,8]{1,2,0:T(8,128)(2,1)S(1)}, u32[]{:S(2)}, u32[]{:S(2)}) async-start(bf16[320,144,8]{1,2,0:T(8,128)(2,1)} %copy.88), calls=%async_computation.4 | async-start | bytes 2621440 | tf_op jit(solution)/shard_map/all_to_all | solution.py:133
  (50 other events, 108.0 us)
where the time goes:
time: 1120 us
  other arithmetic  782 us (70%)
  starting transfers between devices  93.9 us (8%)
  waiting for transfers between devices  83.6 us (7%)
  local copies, waits for them, and re-layouts  58 us (5%)
  matrix products  54.2 us (5%)
  blocking collectives  39.9 us (4%)
    convert_element_type x13, other arithmetic, one_block(): jnp.where(active, block_cos, 0.0).astype(jnp.bfloat16)  728 us
    all_to_all x1, starting transfers between devices, on_device(): lax.all_to_all(partial_back, 'wave', split_axis=0, concat_axis=2, tiled=T...  70.8 us
    dot_general x13, matrix products, one_block(): lax.dot_general(tendency.reshape(3 * levels, block_width), tables, (((1,)...  38 us
    all_to_all x1, waiting for transfers between devices, on_device(): lax.all_to_all(partial_back, 'wave', split_axis=0, concat_axis=2, tiled=T...  31.5 us
    all_to_all x1, blocking collectives, on_device(): lax.all_to_all(spec_local, 'lev', split_axis=3, concat_axis=0, tiled=True)  26.3 us
  transfers between devices with their start and end apart: 4, of which 4 were waited for; matrix products, arithmetic and copies ran while one was open for 1% of the time, Pallas kernels for 0%

commit v1 on v0

v1 whole, which is shorter than its diff:
```python
import functools

import jax
import jax.numpy as jnp
from jax import lax
from jax.experimental import pallas as pl
from jax.experimental.pallas import tpu as pltpu
from jax.sharding import PartitionSpec as P

PBUF = 5376
BLOCK = 768
LANES = 128

adiabatic_exponent = 2.0 / 7.0

cos_terms = (0.9999999857, -19.73920338, 64.9390589, -85.44903786, 60.15837722, -25.93212729, 6.478082977)
sin_terms = (6.283185301, -41.34169993, 81.60510632, -76.70254382, 42.02196627, -14.88466424, 3.21649078)


def turn_cos_sin(turns):
    square = turns * turns
    cosine = jnp.full_like(turns, cos_terms[-1])
    for term in cos_terms[-2::-1]:
        cosine = cosine * square + term
    sine = jnp.full_like(turns, sin_terms[-1])
    for term in sin_terms[-2::-1]:
        sine = sine * square + term
    return cosine, sine * turns


def turns_of(product, count, inverse):
    return (product - count * jnp.round(product * inverse)) * inverse


def table_kernel(points_ref, waves_ref, table_ref):
    row = pl.program_id(0)
    count = points_ref[row].astype(jnp.float32)
    inverse = 1.0 / jnp.full((1, 1), count, jnp.float32)
    waves_all = waves_ref.shape[0]
    chunk = 64

    def one_chunk(index, carry):
        at = pl.multiple_of(index * chunk, chunk)
        waves = waves_ref[pl.ds(at, chunk), :]
        lane = lax.broadcasted_iota(jnp.int32, (chunk, LANES), 1).astype(jnp.float32)
        cosine, sine = turn_cos_sin(turns_of(waves * lane, count, inverse))
        step_cos, step_sin = turn_cos_sin(turns_of(waves * float(LANES), count, inverse))
        for piece in range(BLOCK // LANES):
            where = pl.ds(piece * LANES, LANES)
            table_ref[0, 0, pl.ds(at, chunk), where] = cosine.astype(jnp.bfloat16)
            table_ref[0, 1, pl.ds(at, chunk), where] = (-sine).astype(jnp.bfloat16)
            if piece + 1 < BLOCK // LANES:
                cosine, sine = (
                    cosine * step_cos - sine * step_sin,
                    sine * step_cos + cosine * step_sin,
                )
        return carry

    lax.fori_loop(0, waves_all // chunk, one_chunk, 0)


def make_tables(points, waves):
    rows, waves_all = points.shape[0], waves.shape[0]
    spread = jnp.broadcast_to(waves.astype(jnp.float32)[:, None], (waves_all, LANES))
    return pl.pallas_call(
        table_kernel,
        grid=(rows,),
        out_shape=jax.ShapeDtypeStruct((rows, 2, waves_all, BLOCK), jnp.bfloat16),
        in_specs=[
            pl.BlockSpec(memory_space=pltpu.SMEM),
            pl.BlockSpec((waves_all, LANES), lambda i: (0, 0)),
        ],
        out_specs=pl.BlockSpec((1, 2, waves_all, BLOCK), lambda i: (i, 0, 0, 0)),
        compiler_params=pltpu.CompilerParams(vmem_limit_bytes=40 * 1024 * 1024),
        cost_estimate=pl.CostEstimate(
            flops=rows * waves_all * BLOCK * 40,
            bytes_accessed=rows * waves_all * BLOCK * 4,
            transcendentals=0,
        ),
        name="tables",
    )(points, spread)


def running_sum(values):
    place = lax.broadcasted_iota(jnp.int32, (8, values.shape[1]), 0)
    before = jnp.zeros((1, values.shape[1]), jnp.float32)
    groups = []
    for start in range(0, values.shape[0], 8):
        part = values[start : start + 8]
        for shift in (1, 2, 4):
            part = part + jnp.where(place >= shift, pltpu.roll(part, shift, 0), 0.0)
        part = part + before
        before = part[7:8]
        groups.append(part)
    return jnp.concatenate(groups, axis=0)


def row_kernel(
    points_ref, scale_ref, waves_ref, thick_ref, press_ref, fourier_ref, table_ref,
    back_ref, temp_ref, rotated, grid_part, tend,
):
    row = pl.program_id(0)
    count_int = points_ref[row]
    count = count_int.astype(jnp.float32)
    inverse = 1.0 / jnp.full((1, 1), count, jnp.float32)
    waves = waves_ref[...].astype(jnp.float32)
    waves_all = waves.shape[1]
    fields = fourier_ref.shape[1] // 2
    levels = fields // 3
    blocks = PBUF // BLOCK
    kept = 2.0 * waves < count
    weight = jnp.where(kept, jnp.where(waves == 0.0, 1.0, 2.0), 0.0)
    values = fourier_ref[0].astype(jnp.float32) * weight
    real, imag = values[:fields], values[fields:]

    starts = lax.broadcasted_iota(jnp.int32, (8, waves_all), 0).astype(jnp.float32) * float(BLOCK)
    phase_cos, phase_sin = turn_cos_sin(turns_of(waves * starts, count, inverse))
    for block in range(blocks):
        cosine = phase_cos[block : block + 1]
        sine = phase_sin[block : block + 1]
        there = pl.ds(block * fields, fields)
        rotated[there, :waves_all] = real * cosine - imag * sine
        rotated[there, waves_all:] = real * sine + imag * cosine

    left = rotated[...].astype(jnp.bfloat16)
    for at in range(0, BLOCK, 256):
        right = table_ref[0, :, :, at : at + 256].reshape(2 * waves_all, 256)
        grid_part[:, at : at + 256] = jnp.dot(left, right, preferred_element_type=jnp.float32)

    thick = thick_ref[...]
    factor = adiabatic_exponent / press_ref[...]
    place = lax.broadcasted_iota(jnp.int32, (levels, BLOCK), 1)
    for block in range(blocks):
        inside = place < count_int - block * BLOCK
        vorticity = grid_part[pl.ds(block * fields, levels), :]
        spreading = grid_part[pl.ds(block * fields + levels, levels), :]
        thermal = grid_part[pl.ds(block * fields + 2 * levels, levels), :]
        lifting = -running_sum(thick * spreading)
        first = jnp.where(inside, -vorticity * spreading, 0.0)
        second = jnp.where(inside, 0.5 * (vorticity * vorticity - spreading * spreading), 0.0)
        third = jnp.where(inside, thermal * (factor * lifting - spreading), 0.0)
        tend[pl.ds(block * fields, levels), :] = first
        tend[pl.ds(block * fields + levels, levels), :] = second
        tend[pl.ds(block * fields + 2 * levels, levels), :] = third
        temp_ref[0, :, pl.ds(block * BLOCK, BLOCK)] = third.astype(jnp.bfloat16)

    left = tend[...].astype(jnp.bfloat16)
    scale = scale_ref[row]
    nt = (((1,), (1,)), ((), ()))
    for at in range(0, waves_all, 256):
        lanes = slice(at, at + 256)
        even = lax.dot_general(left, table_ref[0, 0, lanes, :], nt, preferred_element_type=jnp.float32)
        odd = lax.dot_general(left, table_ref[0, 1, lanes, :], nt, preferred_element_type=jnp.float32)
        real_sum = jnp.zeros((fields, 256), jnp.float32)
        imag_sum = jnp.zeros((fields, 256), jnp.float32)
        for block in range(blocks):
            cosine = phase_cos[block : block + 1, lanes]
            sine = phase_sin[block : block + 1, lanes]
            rows = slice(block * fields, (block + 1) * fields)
            real_sum += cosine * even[rows] + sine * odd[rows]
            imag_sum += cosine * odd[rows] - sine * even[rows]
        keep = jnp.where(kept[:, lanes], scale, 0.0)
        back_ref[0, :fields, lanes] = (real_sum * keep).astype(jnp.bfloat16)
        back_ref[0, fields:, lanes] = (imag_sum * keep).astype(jnp.bfloat16)


def row_trips(fourier, tables, waves, points, scales, thickness):
    rows, columns, waves_all = fourier.shape
    levels = thickness.shape[0]
    pressure = jnp.cumsum(thickness) - 0.5 * thickness
    stacked = PBUF // BLOCK * columns // 2
    whole = lambda i: (0, 0)
    return pl.pallas_call(
        row_kernel,
        grid=(rows,),
        out_shape=(
            jax.ShapeDtypeStruct((rows, columns, waves_all), jnp.bfloat16),
            jax.ShapeDtypeStruct((rows, levels, PBUF), jnp.bfloat16),
        ),
        in_specs=[
            pl.BlockSpec(memory_space=pltpu.SMEM),
            pl.BlockSpec(memory_space=pltpu.SMEM),
            pl.BlockSpec((1, waves_all), whole),
            pl.BlockSpec((levels, 1), whole),
            pl.BlockSpec((levels, 1), whole),
            pl.BlockSpec((1, columns, waves_all), lambda i: (i, 0, 0)),
            pl.BlockSpec((1, 2, waves_all, BLOCK), lambda i: (i, 0, 0, 0)),
        ],
        out_specs=(
            pl.BlockSpec((1, columns, waves_all), lambda i: (i, 0, 0)),
            pl.BlockSpec((1, levels, PBUF), lambda i: (i, 0, 0)),
        ),
        scratch_shapes=[
            pltpu.VMEM((stacked, 2 * waves_all), jnp.float32),
            pltpu.VMEM((stacked, BLOCK), jnp.float32),
            pltpu.VMEM((stacked, BLOCK), jnp.float32),
        ],
        compiler_params=pltpu.CompilerParams(vmem_limit_bytes=56 * 1024 * 1024),
        cost_estimate=pl.CostEstimate(
            flops=rows * stacked * waves_all * 2 * BLOCK * 4,
            bytes_accessed=rows * waves_all * BLOCK * 4,
            transcendentals=0,
        ),
        name="rows",
    )(points, scales, waves[None, :], thickness[:, None], pressure[:, None], fourier, tables)


def on_device(spectral, legendre, wave_map, row_map, points, row_weight, thickness):
    wave_count = lax.axis_size("wave")
    level_count = lax.axis_size("lev")
    device_count = wave_count * level_count
    device_flat = lax.axis_index("wave") * level_count + lax.axis_index("lev")
    slots_here = legendre.shape[0]
    waves_all = wave_map.shape[0]
    rows_all = row_map.shape[0]
    rows_here = rows_all // device_count
    levels = thickness.shape[0]
    columns = 6 * levels
    arrival_waves = (
        wave_map.reshape(wave_count, level_count, slots_here).transpose(1, 0, 2).reshape(-1)
    )
    owned_rows = lax.dynamic_slice_in_dim(row_map, device_flat * rows_here, rows_here)
    owned_points = jnp.take(points, owned_rows)
    owned_scales = jnp.take(row_weight, owned_rows) / owned_points.astype(jnp.float32)
    tables = make_tables(owned_points, arrival_waves)

    slot_coefs = lax.all_to_all(spectral, "lev", split_axis=0, concat_axis=3, tiled=True)
    local_waves = lax.dynamic_slice_in_dim(wave_map, device_flat * slots_here, slots_here)
    kept_mask = jnp.arange(waves_all, dtype=jnp.int32)[None, :] < (waves_all - local_waves)[:, None]
    masked_coefs = jnp.where(
        kept_mask[:, None, None, None, :], slot_coefs, jnp.zeros((), jnp.bfloat16)
    )
    fourier = jnp.einsum(
        "sfplk,skr->sfplr", masked_coefs, legendre, preferred_element_type=jnp.float32
    ).astype(jnp.bfloat16)
    fourier = fourier.transpose(0, 2, 1, 3, 4).reshape(slots_here, columns, rows_all)
    outgoing = jnp.take(fourier, row_map, axis=2)
    arrived = lax.all_to_all(
        lax.all_to_all(outgoing, "wave", split_axis=2, concat_axis=0, tiled=True),
        "lev",
        split_axis=2,
        concat_axis=0,
        tiled=True,
    )
    by_row = arrived.transpose(2, 1, 0)
    row_backs, row_temps = row_trips(
        by_row, tables, arrival_waves, owned_points, owned_scales, thickness
    )
    returning = row_backs.transpose(2, 1, 0)
    partial_back = lax.all_to_all(returning, "lev", split_axis=0, concat_axis=2, tiled=True)
    gathered = lax.all_to_all(partial_back, "wave", split_axis=0, concat_axis=2, tiled=True)
    positions = (
        jnp.zeros((rows_all,), jnp.int32).at[row_map].set(jnp.arange(rows_all, dtype=jnp.int32))
    )
    by_latitude = jnp.take(gathered, positions, axis=2)
    direct_sums = jnp.einsum(
        "scr,skr->sck", by_latitude, legendre, preferred_element_type=jnp.float32
    )
    spec_local = (
        jnp.where(kept_mask[:, None, :], direct_sums, 0.0)
        .astype(jnp.bfloat16)
        .reshape(slots_here, 2, 3, levels, waves_all)
        .transpose(0, 2, 1, 3, 4)
    )
    spec_tend = lax.all_to_all(spec_local, "lev", split_axis=3, concat_axis=0, tiled=True)
    return (spec_tend, row_temps)


def solution(mesh):
    return jax.shard_map(
        on_device,
        mesh=mesh,
        in_specs=(
            P("wave", None, None, "lev", None),
            P(("wave", "lev"), None, None),
            P(),
            P(),
            P(),
            P(),
            P(),
        ),
        out_specs=(P("wave", None, None, "lev", None), P(("wave", "lev"), None, None)),
        check_vma=False,
    )
```

time: 1120 us -> 231 us (0.21)
  other arithmetic: 782 us -> 8.88 us
  starting transfers between devices: 93.9 us -> 30.6 us
  matrix products: 54.2 us -> 6.66 us
  Pallas kernels: 0 us -> 20.3 us
  local copies, waits for them, and re-layouts: 58 us -> 42.6 us
    convert_element_type x30 -> x1, other arithmetic: 730 us -> 0.6 us  [make_tables(): waves.astype(jnp.float32)[:, None]]
    all_to_all x1, starting transfers between devices: 70.8 us -> 7.43 us  [on_device(): lax.all_to_all(partial_back, 'wave', split_axis=0, concat_axis=2, tiled=T...]
    dot_general x26 -> x0, matrix products: 47.6 us -> none  [the longest x13 38 us: one_block(): lax.dot_general(tendency.reshape(3 * levels, block_width), tables, (((1,)...]
    pallas_call x0 -> x2, Pallas kernels: none -> 20.3 us  [the longest x1 14.5 us: row_trips(): pl.pallas_call(row_kernel, grid=(rows,), out_shape=(jax.ShapeDtypeStruct(...]
    cos x13 -> x0, other arithmetic: 12 us -> none  [one_block(): phase_cos = jnp.cos(phase)[:, None]]
  transfers between devices with their start and end apart: 4 -> 4, of which waited for: 4 -> 3; matrix products, arithmetic and copies ran while one was open for 1% -> 4% of each run, Pallas kernels for 0% -> 2%
where the time goes in v1:
time: 231 us; the launch traced here: 230 us
  waiting for transfers between devices  72.9 us (32%)
  blocking collectives  47.1 us (20%)
  local copies, waits for them, and re-layouts  42.6 us (18%)
  starting transfers between devices  30.6 us (13%)
  Pallas kernels  20.3 us (9%)
  other arithmetic  8.88 us (4%)
  matrix products  6.66 us (3%)
    all_to_all x1, waiting for transfers between devices, on_device(): lax.all_to_all(partial_back, 'wave', split_axis=0, concat_axis=2, tiled=T...  31.3 us
    all_to_all x1, blocking collectives, on_device(): lax.all_to_all(spec_local, 'lev', split_axis=3, concat_axis=0, tiled=True)  26.3 us
    all_to_all x1, waiting for transfers between devices, on_device(): lax.all_to_all(spectral, 'lev', split_axis=0, concat_axis=3, tiled=True)  21.7 us
    all_to_all x1, blocking collectives, on_device(): lax.all_to_all(returning, 'lev', split_axis=0, concat_axis=2, tiled=True)  20.8 us
    all_to_all x1, waiting for transfers between devices, on_device(): lax.all_to_all(outgoing, 'wave', split_axis=2, concat_axis=0, tiled=True)  19.9 us
    pallas_call x1, Pallas kernels, row_trips(): pl.pallas_call(row_kernel, grid=(rows,), out_shape=(jax.ShapeDtypeStruct(...  14.5 us
    all_to_all x1, starting transfers between devices, on_device(): lax.all_to_all(outgoing, 'wave', split_axis=2, concat_axis=0, tiled=True)  14.2 us
    unnamed x30, local copies, waits for them, and re-layouts  8.96 us
  transfers between devices with their start and end apart: 4, of which 3 were waited for; matrix products, arithmetic and copies ran while one was open for 4% of the time, Pallas kernels for 2%

profile of v1, /device:TPU:1, one launch (start us, length us, event | category | flops | bytes accessed | tf_op | source)
XLA Modules:
  0.0 230.0 jit_solution(12521296778749322035)
XLA Ops:
  0.7 5.2 %all-to-all-start = ((bf16[20,3,2,6,1280]{4,2,3,1,0:T(2,128)(2,1)}), bf16[20,3,2,6,1280]{4,2,3,1,0:T(2,128)(2,1)S(1)}, u32[]{:S(2)}, u32[]{:S(2)}) async-start(bf16[20,3,2,6,1280]{4,2,3,1,0:T(2,128)(2,1)} %param.9), calls=%async_computation | async-start | bytes 3686400 | tf_op jit(solution)/shard_map/all_to_all | solution.py:227
  6.0 21.7 %all-to-all-done = bf16[20,3,2,6,1280]{4,2,3,1,0:T(2,128)(2,1)S(1)} async-done(((bf16[20,3,2,6,1280]{4,2,3,1,0:T(2,128)(2,1)}), bf16[20,3,2,6,1280]{4,2,3,1,0:T(2,128)(2,1)S(1)}, u32[]{:S(2)}, u32[]{:S(2)}) %all-to-all-start) | async-done | bytes 1843232 | tf_op jit(solution)/shard_map/all_to_all | solution.py:227
  33.8 2.7 %gather_fusion.2 = bf16[512,5,144]{2,1,0:T(8,128)(2,1)} fusion(bf16[5,144,512]{1,0,2:T(8,128)(2,1)S(1)} %copy.98, s32[1024]{0:T(1024)S(1)} %pad_clamp_fusion.1), kind=kCustom, calls=%fused_computation.clone | custom fusion | bytes 1476608 | tf_op jit(solution)/shard_map/jit(_take)/gather | solution.py:237
  36.6 2.9 %fusion.17 = bf16[512,5,144]{2,1,0:T(8,128)(2,1)S(1)} fusion(bf16[512,5,144]{2,1,0:T(8,128)(2,1)} %gather_fusion.2, pred[512]{0:T(512)(128)(4,1)S(1)} %compare_and_fusion.1), kind=kLoop, calls=%fused_computation.35 | loop fusion | flops 368640 | bytes 1475072
  39.5 3.1 %reshape.143 = bf16[64,2,2880]{2,1,0:T(2,128)(2,1)} reshape(bf16[512,5,144]{2,1,0:T(8,128)(2,1)S(1)} %fusion.17) | data formatting | bytes 1474560
  42.5 14.2 %all-to-all-start.1 = ((bf16[64,2,2880]{2,1,0:T(2,128)(2,1)}), bf16[64,2,2880]{2,1,0:T(2,128)(2,1)S(1)}, u32[]{:S(2)}, u32[]{:S(2)}) async-start(bf16[64,2,2880]{2,1,0:T(2,128)(2,1)} %reshape.143), calls=%async_computation.1 | async-start | bytes 1507328 | tf_op jit(solution)/shard_map/all_to_all | solution.py:239
  59.1 19.9 %all-to-all-done.1 = bf16[64,2,2880]{2,1,0:T(2,128)(2,1)S(1)} async-done(((bf16[64,2,2880]{2,1,0:T(2,128)(2,1)}), bf16[64,2,2880]{2,1,0:T(2,128)(2,1)S(1)}, u32[]{:S(2)}, u32[]{:S(2)}) %all-to-all-start.1) | async-done | bytes 737312 | tf_op jit(solution)/shard_map/all_to_all | solution.py:239
  79.0 2.7 %reshape.144 = bf16[512,5,144]{2,1,0:T(8,128)(2,1)S(1)} reshape(bf16[64,2,2880]{2,1,0:T(2,128)(2,1)S(1)} %all-to-all-done.1) | data formatting | bytes 1474560
  83.8 3.8 %all-to-all-start.2 = ((bf16[320,144,8]{0,1,2:T(8,128)(2,1)}), bf16[320,144,8]{0,1,2:T(8,128)(2,1)S(1)}, u32[]{:S(2)}, u32[]{:S(2)}) async-start(bf16[320,144,8]{0,1,2:T(8,128)(2,1)} %copy.100), calls=%async_computation.2 | async-start | bytes 1769472 | tf_op jit(solution)/shard_map/all_to_all | solution.py:238
  91.1 5.7 %tables.1.table_ref = bf16[2,2,1280,768]{3,2,1,0:T(8,128)(2,1)S(1)} custom-call(s32[2]{0:T(128)S(1)} %broadcast_select_fusion.1.points_ref, f32[1280,128]{1,0:T(8,128)S(1)} %broadcast_in_dim.64.waves_ref), custom_call_target="tpu_custom_call" | custom-call | flops 78643200 | bytes 7864320 | tf_op jit(solution)/shard_map/tables/pallas_call | solution.py:65
  96.9 3.0 %copy-done.1 = bf16[2,2,1280,768]{3,2,1,0:T(8,128)(2,1)} copy-done((bf16[2,2,1280,768]{3,2,1,0:T(8,128)(2,1)}, bf16[2,2,1280,768]{3,2,1,0:T(8,128)(2,1)S(1)}, u32[]{:S(2)}) %copy-start.1) | copy-done | bytes 7864344
  102.5 14.5 %rows.1 = (bf16[2,144,1280]{2,1,0:T(8,128)(2,1)}, bf16[2,24,5376]{2,1,0:T(8,128)(2,1)}) custom-call(s32[2]{0:T(128)} %copy-done.2, f32[2]{0:T(128)} %convert_divide_fusion.scale_ref, s32[1,1280]{1,0:T(1,128)} %broadcast_in_dim_reshape.3.waves_ref, f32[24,1]{1,0:T(8,128)} %copy-done.5, f32[24,1]{1,0:T(8,128)} %copy.104.press_ref, ...), custom_call_target="tpu_custom_call" | custom-call | flops 7927234560 | bytes 7864320 | tf_op jit(solution)/shard_map/rows/pallas_call | solution.py:173
  117.1 3.3 %copy.105 = bf16[1280,144,2]{1,2,0:T(2,128)(2,1)S(1)} copy(bf16[1280,144,2]{0,1,2:T(8,128)(2,1)} %bitcast.77) | data formatting | bytes 1474560 | tf_op jit(solution)/shard_map/transpose | solution.py:249
  120.4 20.8 %all_to_all.108 = bf16[1280,144,2]{1,2,0:T(2,128)(2,1)S(1)} all-to-all(bf16[1280,144,2]{1,2,0:T(2,128)(2,1)S(1)} %copy.105), channel_id=1, replica_groups=mesh['wave'=64,'lev'=4] {'lev'}, dimensions={0} | all-to-all | bytes 1474560 | tf_op jit(solution)/shard_map/all_to_all | solution.py:250
  141.2 3.1 %copy.117 = bf16[4,320,144,2]{1,0,2,3:T(4,128)(2,1)S(1)} copy(bf16[4,320,144,2]{2,3,1,0:T(2,128)(2,1)S(1)} %bitcast.68) | data formatting | bytes 1474560 | tf_op jit(solution)/shard_map/all_to_all | solution.py:250
  144.4 1.9 copy.108
  146.3 7.4 %all-to-all-start.4 = ((bf16[320,144,8]{1,2,0:T(8,128)(2,1)}), bf16[320,144,8]{1,2,0:T(8,128)(2,1)S(1)}, u32[]{:S(2)}, u32[]{:S(2)}) async-start(bf16[320,144,8]{1,2,0:T(8,128)(2,1)} %copy.108), calls=%async_computation.4 | async-start | bytes 2621440 | tf_op jit(solution)/shard_map/all_to_all | solution.py:251
  153.7 2.8 %scatter_custom_fusion = s32[512]{0:T(512)S(1)} fusion(s32[512]{0:T(512)} %copy-done.10, s32[512]{0:T(512)S(1)} %iota.14, s32[]{:T(128)} %constant.39.clone.1), kind=kCustom, calls=%fused_computation.29 | custom fusion | bytes 2560 | tf_op jit(solution)/shard_map/scatter | solution.py:253
  156.5 31.3 %all-to-all-done.4 = bf16[320,144,8]{1,2,0:T(8,128)(2,1)S(1)} async-done(((bf16[320,144,8]{1,2,0:T(8,128)(2,1)}), bf16[320,144,8]{1,2,0:T(8,128)(2,1)S(1)}, u32[]{:S(2)}, u32[]{:S(2)}) %all-to-all-start.4) | async-done | bytes 737312 | tf_op jit(solution)/shard_map/all_to_all | solution.py:251
  188.0 2.2 copy.110
  190.1 2.6 %gather_fusion.3 = bf16[512,5,144]{2,1,0:T(8,128)(2,1)S(1)} fusion(bf16[5,144,512]{1,0,2:T(8,128)(2,1)} %copy.110, s32[1024]{0:T(1024)S(1)} %pad_clamp_fusion), kind=kCustom, calls=%fused_computation.1.clone | custom fusion | bytes 1476608 | tf_op jit(solution)/shard_map/jit(_take)/gather | solution.py:255
  194.5 5.3 %fusion.2 = bf16[5,144,1280]{2,1,0:T(8,128)(2,1)S(1)} fusion(bf16[5,1280,512]{2,1,0:T(8,128)(2,1)} %param.10, pred[5,1280]{1,0:T(8,128)(4,1)S(1)} %iota_compare_fusion, bf16[5,144,512]{1,0,2:T(8,128)(2,1)S(1)} %select_bitcast_fusion), kind=kOutput, calls=%fused_computation.9 | convolution fusion | flops 945561600 | bytes 9140480 | tf_op jit(solution)/shard_map/scr,skr->sck/dot_general | solution.py:256
  201.2 26.3 %all_to_all.109 = bf16[5,3,2,24,1280]{4,2,1,0,3:T(2,128)(2,1)S(1)} all-to-all(bf16[5,3,2,24,1280]{4,2,1,0,3:T(2,128)(2,1)S(1)} %bitcast.63), channel_id=1, replica_groups=mesh['wave'=64,'lev'=4] {'lev'}, dimensions={3} | all-to-all | bytes 3686400 | tf_op jit(solution)/shard_map/all_to_all | solution.py:265
  227.5 2.5 %copy.114 = bf16[4,5,3,2,6,1280]{5,3,4,2,1,0:T(2,128)(2,1)} copy(bf16[4,5,3,2,6,1280]{5,3,2,1,4,0:T(2,128)(2,1)S(1)} %bitcast.64) | data formatting | bytes 3686400 | tf_op jit(solution)/shard_map/all_to_all | solution.py:265
  (69 shorter events, 20.1 us)
Async XLA Ops:
  0.6 87.0 %copy-start = (s32[512]{0:T(512)S(1)}, s32[512]{0:T(512)}, u32[]{:S(2)}) copy-start(s32[512]{0:T(512)} %param.13) | copy-start | bytes 6148
  0.6 5.2 %copy-start.9 = (s32[1280]{0:T(1024)S(1)}, s32[1280]{0:T(1024)}, u32[]{:S(2)}) copy-start(s32[1280]{0:T(1024)} %param.11) | copy-start | bytes 15364
  0.7 5.3 %copy-start.7 = (s32[512]{0:T(512)S(1)}, s32[512]{0:T(512)}, u32[]{:S(2)}) copy-start(s32[512]{0:T(512)} %param.12) | copy-start | bytes 6148
  0.7 27.0 %all-to-all-start = ((bf16[20,3,2,6,1280]{4,2,3,1,0:T(2,128)(2,1)}), bf16[20,3,2,6,1280]{4,2,3,1,0:T(2,128)(2,1)S(1)}, u32[]{:S(2)}, u32[]{:S(2)}) async-start(bf16[20,3,2,6,1280]{4,2,3,1,0:T(2,128)(2,1)} %param.9), calls=%async_computation | async-start | bytes 3686400 | tf_op jit(solution)/shard_map/all_to_all | solution.py:227
  5.9 24.5 %copy-start.10 = (s32[512]{0:T(512)}, s32[512]{0:T(512)S(1)}, u32[]{:S(2)}) copy-start(s32[512]{0:T(512)S(1)} %compare_select_fusion.1) | copy-start | bytes 6148
  27.7 2.9 %copy-start.4 = (bf16[5,1280,512]{2,1,0:T(8,128)(2,1)S(1)}, bf16[5,1280,512]{2,1,0:T(8,128)(2,1)}, u32[]{:S(2)}) copy-start(bf16[5,1280,512]{2,1,0:T(8,128)(2,1)} %param.10) | copy-start | bytes 19660804
  39.5 17.5 %copy-start.11 = (f32[24]{0:T(128)S(1)}, f32[24]{0:T(128)}, u32[]{:S(2)}) copy-start(f32[24]{0:T(128)} %param.15) | copy-start | bytes 292
  42.5 36.5 %all-to-all-start.1 = ((bf16[64,2,2880]{2,1,0:T(2,128)(2,1)}), bf16[64,2,2880]{2,1,0:T(2,128)(2,1)S(1)}, u32[]{:S(2)}, u32[]{:S(2)}) async-start(bf16[64,2,2880]{2,1,0:T(2,128)(2,1)} %reshape.143), calls=%async_computation.1 | async-start | bytes 1507328 | tf_op jit(solution)/shard_map/all_to_all | solution.py:239
  57.1 24.6 %copy-start.5 = (f32[24,1]{1,0:T(8,128)}, f32[24,1]{1,0:T(8,128)S(1)}, u32[]{:S(2)}) copy-start(f32[24,1]{1,0:T(8,128)S(1)} %copy.103.thick_ref) | copy-start | bytes 292
  82.2 5.5 %copy-start.13 = (s32[2]{0:T(128)S(1)}, s32[2]{0:T(128)}, u32[]{:S(2)}) copy-start(s32[2]{0:T(128)} %compare_select_fusion.2) | copy-start | bytes 28
  82.2 6.1 %copy-start.3 = (f32[512]{0:T(512)S(1)}, f32[512]{0:T(512)}, u32[]{:S(2)}) copy-start(f32[512]{0:T(512)} %param.14) | copy-start | bytes 6148
  83.8 6.0 %copy-start.12 = (f32[24,1]{0,1:T(1,128)S(1)}, f32[24,1]{0,1:T(1,128)}, u32[]{:S(2)}) copy-start(f32[24,1]{0,1:T(1,128)} %subtract_bitcast_fusion) | copy-start | bytes 292
  83.8 6.6 %copy-start.6 = (f32[4,64,5]{1,0,2:T(4,128)S(1)}, f32[4,64,5]{1,0,2:T(4,128)}, u32[]{:S(2)}) copy-start(f32[4,64,5]{1,0,2:T(4,128)} %bitcast_convert_fusion) | copy-start | bytes 15364
  83.8 7.0 %copy-start.8 = (s32[512]{0:T(512)S(1)}, s32[512]{0:T(512)}, u32[]{:S(2)}) copy-start(s32[512]{0:T(512)} %param.12) | copy-start | bytes 6148
  83.8 16.7 %all-to-all-start.2 = ((bf16[320,144,8]{0,1,2:T(8,128)(2,1)}), bf16[320,144,8]{0,1,2:T(8,128)(2,1)S(1)}, u32[]{:S(2)}, u32[]{:S(2)}) async-start(bf16[320,144,8]{0,1,2:T(8,128)(2,1)} %copy.100), calls=%async_computation.2 | async-start | bytes 1769472 | tf_op jit(solution)/shard_map/all_to_all | solution.py:238
  90.9 6.0 %copy-start.2 = (s32[2]{0:T(128)}, s32[2]{0:T(128)S(1)}, u32[]{:S(2)}) copy-start(s32[2]{0:T(128)S(1)} %broadcast_select_fusion.1.points_ref) | copy-start | bytes 28
  96.9 3.1 %copy-start.1 = (bf16[2,2,1280,768]{3,2,1,0:T(8,128)(2,1)}, bf16[2,2,1280,768]{3,2,1,0:T(8,128)(2,1)S(1)}, u32[]{:S(2)}) copy-start(bf16[2,2,1280,768]{3,2,1,0:T(8,128)(2,1)S(1)} %tables.1.table_ref) | copy-start | bytes 23592964
  146.3 41.6 %all-to-all-start.4 = ((bf16[320,144,8]{1,2,0:T(8,128)(2,1)}), bf16[320,144,8]{1,2,0:T(8,128)(2,1)S(1)}, u32[]{:S(2)}, u32[]{:S(2)}) async-start(bf16[320,144,8]{1,2,0:T(8,128)(2,1)} %copy.108), calls=%async_computation.4 | async-start | bytes 2621440 | tf_op jit(solution)/shard_map/all_to_all | solution.py:251

commit v2 on v1

--- a/solution.py
+++ b/solution.py
@@ -1,7 +1,6 @@
-import functools
-
 import jax
 import jax.numpy as jnp
+import numpy as np
 from jax import lax
 from jax.experimental import pallas as pl
 from jax.experimental.pallas import tpu as pltpu
@@ -10,6 +9,10 @@
 PBUF = 5376
 BLOCK = 768
 LANES = 128
+MESH = pl.DeviceIdType.MESH
+NT = (((1,), (1,)), ((), ()))
+TN = (((0,), (0,)), ((), ()))
+MIB = 1024 * 1024
 
 adiabatic_exponent = 2.0 / 7.0
 
@@ -95,9 +98,391 @@
     return jnp.concatenate(groups, axis=0)
 
 
+def meet(axis_count, peer_of):
+    barrier = pltpu.get_barrier_semaphore()
+
+    def tell(step, carry):
+        pl.semaphore_signal(barrier, inc=1, device_id=peer_of(step), device_id_type=MESH)
+        return carry
+
+    lax.fori_loop(1, axis_count, tell, 0)
+    return barrier
+
+
+def lev_peer(step):
+    level = lax.axis_index("lev")
+    return lax.axis_index("wave"), lax.rem(level + step, lax.axis_size("lev"))
+
+
+def row_choice(rows_ref):
+    rows_all = rows_ref.shape[1]
+    return jnp.where(
+        lax.broadcasted_iota(jnp.int32, (rows_all, rows_all), 0) == rows_ref[...], 1.0, 0.0
+    ).astype(jnp.bfloat16)
+
+
+def spread_kernel(
+    waves_ref, rows_ref, spec_ref, legendre_ref, out_ref,
+    recv, table, choice, stage, own_sem, table_sem, send_sem, recv_sem, send2_sem, recv2_sem,
+):
+    slots, groups = recv.shape[0], recv.shape[1]
+    waves_all = recv.shape[-1]
+    wave, level = lax.axis_index("wave"), lax.axis_index("lev")
+    loads = [
+        pltpu.make_async_copy(legendre_ref.at[s], table.at[s], table_sem.at[s]) for s in range(slots)
+    ]
+    own = [
+        pltpu.make_async_copy(spec_ref.at[level * slots + s], recv.at[s, level], own_sem.at[s])
+        for s in range(slots)
+    ]
+    barrier = meet(groups, lev_peer)
+    own[0].start()
+    loads[0].start()
+    choice[...] = row_choice(rows_ref)
+    pl.semaphore_wait(barrier, groups - 1)
+
+    first, second = {}, {}
+    for s in range(slots):
+        for step in range(1, groups):
+            peer = lax.rem(level + step, groups)
+            first[s, step] = pltpu.make_async_remote_copy(
+                src_ref=spec_ref.at[peer * slots + s],
+                dst_ref=recv.at[s, level],
+                send_sem=send_sem.at[s, step - 1],
+                recv_sem=recv_sem.at[s, step - 1],
+                device_id=(wave, peer),
+                device_id_type=MESH,
+            )
+            first[s, step].start()
+    for s in range(1, slots):
+        own[s].start()
+        loads[s].start()
+
+    position = lax.broadcasted_iota(jnp.int32, (1, waves_all), 1)
+    for s in range(slots):
+        own[s].wait()
+        for step in range(1, groups):
+            first[s, step].wait_recv()
+        loads[s].wait()
+        coefs = recv[s].reshape(-1, waves_all)
+        keep = jnp.where(position < waves_all - waves_ref[s], 1.0, 0.0)
+        coefs = coefs * jnp.broadcast_to(keep, coefs.shape).astype(jnp.bfloat16)
+        fourier = jnp.dot(coefs, table[s], preferred_element_type=jnp.float32).astype(jnp.bfloat16)
+        placed = jnp.dot(fourier, choice[...], preferred_element_type=jnp.float32).astype(jnp.bfloat16)
+        for group in range(groups):
+            stage[s, group] = placed[:, group * LANES : (group + 1) * LANES]
+        for step in range(1, groups):
+            peer = lax.rem(level + step, groups)
+            second[s, step] = pltpu.make_async_remote_copy(
+                src_ref=stage.at[s, peer],
+                dst_ref=out_ref.at[level, s],
+                send_sem=send2_sem.at[s, step - 1],
+                recv_sem=recv2_sem.at[s, step - 1],
+                device_id=(wave, peer),
+                device_id_type=MESH,
+            )
+            second[s, step].start()
+        out_ref[level, s] = stage[s, level]
+    for copy in list(first.values()) + list(second.values()):
+        copy.wait_send()
+    for copy in second.values():
+        copy.wait_recv()
+
+
+def spread(spec, legendre, local_waves, placed_rows):
+    slots, waves_all, rows_all = legendre.shape
+    groups = spec.shape[0] // slots
+    pairs = spec.shape[1]
+    columns = groups * pairs * 2
+    dma = pltpu.SemaphoreType.DMA
+    return pl.pallas_call(
+        spread_kernel,
+        out_shape=jax.ShapeDtypeStruct((groups, slots, columns, LANES), jnp.bfloat16),
+        in_specs=[
+            pl.BlockSpec(memory_space=pltpu.SMEM),
+            pl.BlockSpec(memory_space=pltpu.VMEM),
+            pl.BlockSpec(memory_space=pl.ANY),
+            pl.BlockSpec(memory_space=pl.ANY),
+        ],
+        out_specs=pl.BlockSpec(memory_space=pltpu.VMEM),
+        scratch_shapes=[
+            pltpu.VMEM((slots, groups, pairs, 2, waves_all), jnp.bfloat16),
+            pltpu.VMEM((slots, waves_all, rows_all), jnp.bfloat16),
+            pltpu.VMEM((rows_all, rows_all), jnp.bfloat16),
+            pltpu.VMEM((slots, groups, columns, LANES), jnp.bfloat16),
+            dma((slots,)),
+            dma((slots,)),
+            dma((slots, groups - 1)),
+            dma((slots, groups - 1)),
+            dma((slots, groups - 1)),
+            dma((slots, groups - 1)),
+        ],
+        compiler_params=pltpu.CompilerParams(
+            collective_id=1, has_side_effects=True, vmem_limit_bytes=48 * MIB
+        ),
+        cost_estimate=pl.CostEstimate(
+            flops=2 * slots * columns * rows_all * (waves_all + rows_all),
+            bytes_accessed=slots * waves_all * rows_all * 2,
+            transcendentals=0,
+        ),
+        name="spread",
+    )(local_waves, placed_rows, spec, legendre)
+
+
+def gather_kernel(
+    waves_ref, rows_ref, x_ref, legendre_ref, out_ref,
+    recv, table, choice, stage, table_sem, own_sem, send_sem, recv_sem, send2_sem, recv2_sem,
+):
+    groups, slots, columns, _ = recv.shape
+    waves_all = table.shape[1]
+    wave, level = lax.axis_index("wave"), lax.axis_index("lev")
+    loads = [
+        pltpu.make_async_copy(legendre_ref.at[s], table.at[s], table_sem.at[s]) for s in range(slots)
+    ]
+    barrier = meet(groups, lev_peer)
+    loads[0].start()
+    recv[level] = x_ref[level]
+    choice[...] = row_choice(rows_ref)
+    pl.semaphore_wait(barrier, groups - 1)
+
+    first, second, own = {}, {}, {}
+    for s in range(slots):
+        for step in range(1, groups):
+            peer = lax.rem(level + step, groups)
+            first[s, step] = pltpu.make_async_remote_copy(
+                src_ref=x_ref.at[peer, s],
+                dst_ref=recv.at[level, s],
+                send_sem=send_sem.at[s, step - 1],
+                recv_sem=recv_sem.at[s, step - 1],
+                device_id=(wave, peer),
+                device_id_type=MESH,
+            )
+            first[s, step].start()
+    for s in range(1, slots):
+        loads[s].start()
+
+    position = lax.broadcasted_iota(jnp.int32, (1, waves_all), 1)
+    for s in range(slots):
+        for step in range(1, groups):
+            first[s, step].wait_recv()
+        loads[s].wait()
+        placed = jnp.concatenate([recv[group, s] for group in range(groups)], axis=1)
+        back = lax.dot_general(placed, choice[...], NT, preferred_element_type=jnp.float32)
+        sums = lax.dot_general(
+            back.astype(jnp.bfloat16), table[s], NT, preferred_element_type=jnp.float32
+        )
+        sums = jnp.where(position < waves_all - waves_ref[s], sums, 0.0).astype(jnp.bfloat16)
+        stage[s] = sums.reshape(stage.shape[1:])
+        for step in range(1, groups):
+            peer = lax.rem(level + step, groups)
+            second[s, step] = pltpu.make_async_remote_copy(
+                src_ref=stage.at[s, peer],
+                dst_ref=out_ref.at[level * slots + s],
+                send_sem=send2_sem.at[s, step - 1],
+                recv_sem=recv2_sem.at[s, step - 1],
+                device_id=(wave, peer),
+                device_id_type=MESH,
+            )
+            second[s, step].start()
+        own[s] = pltpu.make_async_copy(
+            stage.at[s, level], out_ref.at[level * slots + s], own_sem.at[s]
+        )
+        own[s].start()
+    for copy in list(first.values()) + list(second.values()):
+        copy.wait_send()
+    for copy in second.values():
+        copy.wait_recv()
+    for copy in own.values():
+        copy.wait()
+
+
+def gather(x, legendre, local_waves, placed_rows):
+    slots, waves_all, rows_all = legendre.shape
+    groups, _, columns, _ = x.shape
+    pairs = columns // groups // 2
+    dma = pltpu.SemaphoreType.DMA
+    return pl.pallas_call(
+        gather_kernel,
+        out_shape=jax.ShapeDtypeStruct((groups * slots, pairs, 2, waves_all), jnp.bfloat16),
+        in_specs=[
+            pl.BlockSpec(memory_space=pltpu.SMEM),
+            pl.BlockSpec(memory_space=pltpu.VMEM),
+            pl.BlockSpec(memory_space=pltpu.VMEM),
+            pl.BlockSpec(memory_space=pl.ANY),
+        ],
+        out_specs=pl.BlockSpec(memory_space=pl.ANY),
+        scratch_shapes=[
+            pltpu.VMEM((groups, slots, columns, LANES), jnp.bfloat16),
+            pltpu.VMEM((slots, waves_all, rows_all), jnp.bfloat16),
+            pltpu.VMEM((rows_all, rows_all), jnp.bfloat16),
+            pltpu.VMEM((slots, groups, pairs, 2, waves_all), jnp.bfloat16),
+            dma((slots,)),
+            dma((slots,)),
+            dma((slots, groups - 1)),
+            dma((slots, groups - 1)),
+            dma((slots, groups - 1)),
+            dma((slots, groups - 1)),
+        ],
+        compiler_params=pltpu.CompilerParams(
+            collective_id=2, has_side_effects=True, vmem_limit_bytes=48 * MIB
+        ),
+        cost_estimate=pl.CostEstimate(
+            flops=2 * slots * columns * rows_all * (waves_all + rows_all),
+            bytes_accessed=slots * waves_all * rows_all * 2,
+            transcendentals=0,
+        ),
+        name="gather",
+    )(local_waves, placed_rows, x, legendre)
+
+
+def wave_peer(step):
+    wave = lax.axis_index("wave")
+    core, z, x = lax.rem(wave, 2), lax.rem(lax.div(wave, 2), 8), lax.div(wave, 16)
+    z = lax.rem(z + lax.rem(step, 8), 8)
+    x = lax.rem(x + lax.rem(lax.div(step, 8), 4), 4)
+    core = lax.rem(core + lax.div(step, 32), 2)
+    return (x * 8 + z) * 2 + core, lax.axis_index("lev")
+
+
+def exchange(barrier, src, dst, own_sem, send_sem, recv_sem):
+    count = src.shape[0]
+    me = lax.axis_index("wave")
+    own = pltpu.make_async_copy(src.at[me], dst.at[me], own_sem)
+    own.start()
+    pl.semaphore_wait(barrier, count - 1)
+
+    def send(step, carry):
+        peer = wave_peer(step)
+        pltpu.make_async_remote_copy(
+            src_ref=src.at[peer[0]],
+            dst_ref=dst.at[me],
+            send_sem=send_sem,
+            recv_sem=recv_sem,
+            device_id=peer,
+            device_id_type=MESH,
+        ).start()
+        return carry
+
+    lax.fori_loop(1, count, send, 0)
+    own.wait()
+    sent = src.at[pl.ds(0, count - 1)]
+    pltpu.make_async_copy(sent, sent, send_sem).wait()
+    come = dst.at[pl.ds(0, count - 1)]
+    pltpu.make_async_copy(come, come, recv_sem).wait()
+
+
+def unit(size):
+    rows = lax.broadcasted_iota(jnp.int32, (size, size), 0)
+    return jnp.where(rows == lax.broadcasted_iota(jnp.int32, (size, size), 1), 1.0, 0.0).astype(jnp.bfloat16)
+
+
+def scatter_rows_kernel(x_ref, out_ref, padded, wide, send, own_sem, send_sem, recv_sem):
+    groups, slots, columns, _ = x_ref.shape
+    waves, lines, _ = out_ref.shape
+    barrier = meet(waves, wave_peer)
+    used = slots * columns
+    tiles = padded.shape[0] // LANES
+    rows_here = LANES // waves
+    padded[pl.ds(used, padded.shape[0] - used), :] = jnp.zeros((padded.shape[0] - used, LANES), jnp.bfloat16)
+    identity = unit(LANES)
+    for group in range(groups):
+        padded[:used, :] = x_ref[group].reshape(used, LANES)
+        turned = lax.dot_general(identity, padded[...], NT, preferred_element_type=jnp.float32)
+        for i in range(rows_here):
+            for tile in range(tiles):
+                line = (group * rows_here + i) * tiles + tile
+                wide[pl.ds(line, waves, stride=lines), :] = turned[
+                    i * waves : (i + 1) * waves, tile * LANES : (tile + 1) * LANES
+                ]
+    send[...] = wide[...].reshape(waves, lines, LANES).astype(jnp.bfloat16)
+    exchange(barrier, send, out_ref, own_sem, send_sem, recv_sem)
+
+
+def scatter_rows(x, waves):
+    groups, slots, columns, _ = x.shape
+    tiles = pl.cdiv(slots * columns, LANES)
+    lines = groups * LANES // waves * tiles
+    dma = pltpu.SemaphoreType.DMA
+    return pl.pallas_call(
+        scatter_rows_kernel,
+        out_shape=jax.ShapeDtypeStruct((waves, lines, LANES), jnp.bfloat16),
+        in_specs=[pl.BlockSpec(memory_space=pltpu.VMEM)],
+        out_specs=pl.BlockSpec(memory_space=pltpu.VMEM),
+        scratch_shapes=[
+            pltpu.VMEM((tiles * LANES, LANES), jnp.bfloat16),
+            pltpu.VMEM((waves * lines, LANES), jnp.float32),
+            pltpu.VMEM((waves, lines, LANES), jnp.bfloat16),
+            dma,
+            dma,
+            dma,
+        ],
+        compiler_params=pltpu.CompilerParams(
+            collective_id=3, has_side_effects=True, vmem_limit_bytes=32 * MIB
+        ),
+        name="scatter_rows",
+    )(x)
+
+
+def collect_rows_kernel(x_ref, out_ref, recv, wide, own_sem, send_sem, recv_sem):
+    groups, slots, columns, _ = out_ref.shape
+    waves, lines, _ = x_ref.shape
+    barrier = meet(waves, wave_peer)
+    exchange(barrier, x_ref, recv, own_sem, send_sem, recv_sem)
+    used = slots * columns
+    tiles = pl.cdiv(used, LANES)
+    rows_here = LANES // waves
+    wide[...] = recv[...].astype(jnp.float32).reshape(waves * lines, LANES)
+    identity = unit(LANES)
+    for group in range(groups):
+        parts = []
+        for i in range(rows_here):
+            line = (group * rows_here + i) * tiles
+            parts.append(
+                jnp.concatenate(
+                    [wide[pl.ds(line + tile, waves, stride=lines), :] for tile in range(tiles)], axis=1
+                )
+            )
+        placed = jnp.concatenate(parts, axis=0).astype(jnp.bfloat16)
+        turned = lax.dot_general(placed, identity, TN, preferred_element_type=jnp.float32)
+        out_ref[group] = turned[:used].astype(jnp.bfloat16).reshape(slots, columns, LANES)
+
+
+def collect_rows(x, groups, slots, columns):
+    waves, lines, _ = x.shape
+    dma = pltpu.SemaphoreType.DMA
+    return pl.pallas_call(
+        collect_rows_kernel,
+        out_shape=jax.ShapeDtypeStruct((groups, slots, columns, LANES), jnp.bfloat16),
+        in_specs=[pl.BlockSpec(memory_space=pltpu.VMEM)],
+        out_specs=pl.BlockSpec(memory_space=pltpu.VMEM),
+        scratch_shapes=[
+            pltpu.VMEM((waves, lines, LANES), jnp.bfloat16),
+            pltpu.VMEM((waves * lines, LANES), jnp.float32),
+            dma,
+            dma,
+            dma,
+        ],
+        compiler_params=pltpu.CompilerParams(
+            collective_id=4, has_side_effects=True, vmem_limit_bytes=32 * MIB
+        ),
+        name="collect_rows",
+    )(x)
+
+
+def column_order(slots, levels, groups):
+    columns = 6 * levels
+    inner = levels // groups
+    slot, part, field, group, level = np.meshgrid(
+        *(np.arange(n) for n in (slots, 2, 3, groups, inner)), indexing="ij"
+    )
+    lane = (slot * columns + ((group * 3 + field) * inner + level) * 2 + part).reshape(-1)
+    width = pl.cdiv(slots * columns, LANES) * LANES
+    return (lane[:, None] == np.arange(width)[None, :]).astype(jnp.bfloat16)
+
+
 def row_kernel(
-    points_ref, scale_ref, waves_ref, thick_ref, press_ref, fourier_ref, table_ref,
-    back_ref, temp_ref, rotated, grid_part, tend,
+    points_ref, scale_ref, waves_ref, thick_ref, press_ref, order_ref, come_ref, table_ref,
+    go_ref, temp_ref, wide, leave, backs, rotated, grid_part, tend,
 ):
     row = pl.program_id(0)
     count_int = points_ref[row]
@@ -105,12 +490,44 @@
     inverse = 1.0 / jnp.full((1, 1), count, jnp.float32)
     waves = waves_ref[...].astype(jnp.float32)
     waves_all = waves.shape[1]
-    fields = fourier_ref.shape[1] // 2
+    fields = 3 * thick_ref.shape[0]
     levels = fields // 3
+    columns = 2 * fields
+    senders, lines, _ = come_ref.shape
+    groups = waves_all * columns // (order_ref.shape[0] * senders)
+    slots = order_ref.shape[0] // columns
+    tiles = order_ref.shape[1] // LANES
+    span = groups * senders
+
+    @pl.when(row == 0)
+    def _():
+        wide[...] = come_ref[...].astype(jnp.float32).reshape(senders * lines, LANES)
+
+    def line_of(group, tile):
+        return (group * pl.num_programs(0) + row) * tiles + tile
+
+    placed = jnp.concatenate(
+        [
+            jnp.concatenate(
+                [wide[pl.ds(line_of(group, tile), senders, stride=lines), :] for tile in range(tiles)], axis=1
+            )
+            for group in range(groups)
+        ],
+        axis=0,
+    ).astype(jnp.bfloat16)
+    fourier = jnp.concatenate(
+        [
+            lax.dot_general(
+                order_ref[slot * columns : (slot + 1) * columns, :], placed, NT, preferred_element_type=jnp.float32
+            )
+            for slot in range(slots)
+        ],
+        axis=1,
+    )
     blocks = PBUF // BLOCK
     kept = 2.0 * waves < count
     weight = jnp.where(kept, jnp.where(waves == 0.0, 1.0, 2.0), 0.0)
-    values = fourier_ref[0].astype(jnp.float32) * weight
+    values = fourier * weight
     real, imag = values[:fields], values[fields:]
 
     starts = lax.broadcasted_iota(jnp.int32, (8, waves_all), 0).astype(jnp.float32) * float(BLOCK)
@@ -146,11 +563,10 @@
 
     left = tend[...].astype(jnp.bfloat16)
     scale = scale_ref[row]
-    nt = (((1,), (1,)), ((), ()))
     for at in range(0, waves_all, 256):
         lanes = slice(at, at + 256)
-        even = lax.dot_general(left, table_ref[0, 0, lanes, :], nt, preferred_element_type=jnp.float32)
-        odd = lax.dot_general(left, table_ref[0, 1, lanes, :], nt, preferred_element_type=jnp.float32)
+        even = lax.dot_general(left, table_ref[0, 0, lanes, :], NT, preferred_element_type=jnp.float32)
+        odd = lax.dot_general(left, table_ref[0, 1, lanes, :], NT, preferred_element_type=jnp.float32)
         real_sum = jnp.zeros((fields, 256), jnp.float32)
         imag_sum = jnp.zeros((fields, 256), jnp.float32)
         for block in range(blocks):
@@ -160,21 +576,40 @@
             real_sum += cosine * even[rows] + sine * odd[rows]
             imag_sum += cosine * odd[rows] - sine * even[rows]
         keep = jnp.where(kept[:, lanes], scale, 0.0)
-        back_ref[0, :fields, lanes] = (real_sum * keep).astype(jnp.bfloat16)
-        back_ref[0, fields:, lanes] = (imag_sum * keep).astype(jnp.bfloat16)
-
-
-def row_trips(fourier, tables, waves, points, scales, thickness):
-    rows, columns, waves_all = fourier.shape
+        there = at // 256 * columns
+        backs[there : there + fields, :] = real_sum * keep
+        backs[there + fields : there + columns, :] = imag_sum * keep
+
+    leaving = lax.dot_general(
+        backs[...].astype(jnp.bfloat16), order_ref[...], TN, preferred_element_type=jnp.float32
+    )
+    for group in range(groups):
+        for tile in range(tiles):
+            leave[pl.ds(line_of(group, tile), senders, stride=lines), :] = leaving[
+                group * senders : (group + 1) * senders, tile * LANES : (tile + 1) * LANES
+            ]
+
+    @pl.when(row == pl.num_programs(0) - 1)
+    def _():
+        go_ref[...] = leave[...].reshape(senders, lines, LANES).astype(jnp.bfloat16)
+
+
+def row_trips(come, tables, waves, points, scales, thickness, slots):
+    senders, lines, _ = come.shape
+    rows = points.shape[0]
+    waves_all = waves.shape[0]
     levels = thickness.shape[0]
+    columns = 6 * levels
+    groups = waves_all // (slots * senders)
     pressure = jnp.cumsum(thickness) - 0.5 * thickness
+    order = column_order(slots, levels, groups)
     stacked = PBUF // BLOCK * columns // 2
     whole = lambda i: (0, 0)
     return pl.pallas_call(
         row_kernel,
         grid=(rows,),
         out_shape=(
-            jax.ShapeDtypeStruct((rows, columns, waves_all), jnp.bfloat16),
+            jax.ShapeDtypeStruct(come.shape, jnp.bfloat16),
             jax.ShapeDtypeStruct((rows, levels, PBUF), jnp.bfloat16),
         ),
         in_specs=[
@@ -183,26 +618,30 @@
             pl.BlockSpec((1, waves_all), whole),
             pl.BlockSpec((levels, 1), whole),
             pl.BlockSpec((levels, 1), whole),
-            pl.BlockSpec((1, columns, waves_all), lambda i: (i, 0, 0)),
+            pl.BlockSpec(order.shape, whole),
+            pl.BlockSpec(come.shape, lambda i: (0, 0, 0)),
             pl.BlockSpec((1, 2, waves_all, BLOCK), lambda i: (i, 0, 0, 0)),
         ],
         out_specs=(
-            pl.BlockSpec((1, columns, waves_all), lambda i: (i, 0, 0)),
+            pl.BlockSpec(come.shape, lambda i: (0, 0, 0)),
             pl.BlockSpec((1, levels, PBUF), lambda i: (i, 0, 0)),
         ),
         scratch_shapes=[
+            pltpu.VMEM((senders * lines, LANES), jnp.float32),
+            pltpu.VMEM((senders * lines, LANES), jnp.float32),
+            pltpu.VMEM((slots * columns, groups * senders), jnp.float32),
             pltpu.VMEM((stacked, 2 * waves_all), jnp.float32),
             pltpu.VMEM((stacked, BLOCK), jnp.float32),
             pltpu.VMEM((stacked, BLOCK), jnp.float32),
         ],
-        compiler_params=pltpu.CompilerParams(vmem_limit_bytes=56 * 1024 * 1024),
+        compiler_params=pltpu.CompilerParams(vmem_limit_bytes=56 * MIB),
         cost_estimate=pl.CostEstimate(
             flops=rows * stacked * waves_all * 2 * BLOCK * 4,
             bytes_accessed=rows * waves_all * BLOCK * 4,
             transcendentals=0,
         ),
         name="rows",
-    )(points, scales, waves[None, :], thickness[:, None], pressure[:, None], fourier, tables)
+    )(points, scales, waves[None, :], thickness[:, None], pressure[:, None], jnp.asarray(order), come, tables)
 
 
 def on_device(spectral, legendre, wave_map, row_map, points, row_weight, thickness):
@@ -210,59 +649,32 @@
     level_count = lax.axis_size("lev")
     device_count = wave_count * level_count
     device_flat = lax.axis_index("wave") * level_count + lax.axis_index("lev")
-    slots_here = legendre.shape[0]
-    waves_all = wave_map.shape[0]
-    rows_all = row_map.shape[0]
+    slots_here, waves_all, rows_all = legendre.shape
     rows_here = rows_all // device_count
     levels = thickness.shape[0]
     columns = 6 * levels
     arrival_waves = (
-        wave_map.reshape(wave_count, level_count, slots_here).transpose(1, 0, 2).reshape(-1)
+        wave_map.reshape(wave_count, level_count, slots_here).transpose(2, 1, 0).reshape(-1)
+    )
+    placed_rows = (
+        row_map.reshape(wave_count, level_count, rows_here).transpose(1, 2, 0).reshape(1, rows_all)
     )
     owned_rows = lax.dynamic_slice_in_dim(row_map, device_flat * rows_here, rows_here)
     owned_points = jnp.take(points, owned_rows)
     owned_scales = jnp.take(row_weight, owned_rows) / owned_points.astype(jnp.float32)
+    local_waves = lax.dynamic_slice_in_dim(wave_map, device_flat * slots_here, slots_here)
     tables = make_tables(owned_points, arrival_waves)
 
-    slot_coefs = lax.all_to_all(spectral, "lev", split_axis=0, concat_axis=3, tiled=True)
-    local_waves = lax.dynamic_slice_in_dim(wave_map, device_flat * slots_here, slots_here)
-    kept_mask = jnp.arange(waves_all, dtype=jnp.int32)[None, :] < (waves_all - local_waves)[:, None]
-    masked_coefs = jnp.where(
-        kept_mask[:, None, None, None, :], slot_coefs, jnp.zeros((), jnp.bfloat16)
+    slots_group, _, _, level_here, _ = spectral.shape
+    pairs = spectral.transpose(0, 1, 3, 2, 4).reshape(slots_group, 3 * level_here, 2, waves_all)
+    placed = spread(pairs, legendre, local_waves, placed_rows)
+    come = scatter_rows(placed, wave_count)
+    go, row_temps = row_trips(
+        come, tables, arrival_waves, owned_points, owned_scales, thickness, slots_here
     )
-    fourier = jnp.einsum(
-        "sfplk,skr->sfplr", masked_coefs, legendre, preferred_element_type=jnp.float32
-    ).astype(jnp.bfloat16)
-    fourier = fourier.transpose(0, 2, 1, 3, 4).reshape(slots_here, columns, rows_all)
-    outgoing = jnp.take(fourier, row_map, axis=2)
-    arrived = lax.all_to_all(
-        lax.all_to_all(outgoing, "wave", split_axis=2, concat_axis=0, tiled=True),
-        "lev",
-        split_axis=2,
-        concat_axis=0,
-        tiled=True,
-    )
-    by_row = arrived.transpose(2, 1, 0)
-    row_backs, row_temps = row_trips(
-        by_row, tables, arrival_waves, owned_points, owned_scales, thickness
-    )
-    returning = row_backs.transpose(2, 1, 0)
-    partial_back = lax.all_to_all(returning, "lev", split_axis=0, concat_axis=2, tiled=True)
-    gathered = lax.all_to_all(partial_back, "wave", split_axis=0, concat_axis=2, tiled=True)
-    positions = (
-        jnp.zeros((rows_all,), jnp.int32).at[row_map].set(jnp.arange(rows_all, dtype=jnp.int32))
-    )
-    by_latitude = jnp.take(gathered, positions, axis=2)
-    direct_sums = jnp.einsum(
-        "scr,skr->sck", by_latitude, legendre, preferred_element_type=jnp.float32
-    )
-    spec_local = (
-        jnp.where(kept_mask[:, None, :], direct_sums, 0.0)
-        .astype(jnp.bfloat16)
-        .reshape(slots_here, 2, 3, levels, waves_all)
-        .transpose(0, 2, 1, 3, 4)
-    )
-    spec_tend = lax.all_to_all(spec_local, "lev", split_axis=3, concat_axis=0, tiled=True)
+    placed = collect_rows(go, level_count, slots_here, columns)
+    pairs = gather(placed, legendre, local_waves, placed_rows)
+    spec_tend = pairs.reshape(slots_group, 3, level_here, 2, waves_all).transpose(0, 1, 3, 2, 4)
     return (spec_tend, row_temps)
 
 

time: 231 us -> 166 us (0.72)
  Pallas kernels: 20.3 us -> 148 us
  waiting for transfers between devices: 72.9 us -> 0 us
  blocking collectives: 47.1 us -> 0 us
  starting transfers between devices: 30.6 us -> 0 us
  local copies, waits for them, and re-layouts: 42.6 us -> 13.7 us
  matrix products: 6.66 us -> 0 us
  other arithmetic: 8.88 us -> 3.61 us
    pallas_call x0 -> x4, Pallas kernels: none -> 126 us  [the longest x1 33.8 us: gather(): pl.pallas_call(gather_kernel, out_shape=jax.ShapeDtypeStruct((groups * sl...]
    all_to_all x4 -> x0, waiting for transfers between devices: 72.9 us -> none  [the longest x1 31.3 us: on_device(): lax.all_to_all(partial_back, 'wave', split_axis=0, concat_axis=2, tiled=T...]
    all_to_all x2 -> x0, blocking collectives: 47.1 us -> none  [the longest x1 26.3 us: on_device(): lax.all_to_all(spec_local, 'lev', split_axis=3, concat_axis=0, tiled=True)]
    all_to_all x4 -> x0, starting transfers between devices: 30.6 us -> none  [the longest x1 14.2 us: on_device(): lax.all_to_all(outgoing, 'wave', split_axis=2, concat_axis=0, tiled=True)]
    all_to_all x11 -> x0, local copies, waits for them, and re-layouts: 15.1 us -> none  [the longest x3 5.07 us: on_device(): lax.all_to_all(returning, 'lev', split_axis=0, concat_axis=2, tiled=True)]
    dot_general x2 -> x0, matrix products: 6.66 us -> none  [the longest x1 5.3 us: on_device(): jnp.einsum('scr,skr->sck', by_latitude, legendre, preferred_element_type=...]
    gather x2 -> x0, local copies, waits for them, and re-layouts: 5.3 us -> none  [the longest x1 2.74 us: on_device(): outgoing = jnp.take(fourier, row_map, axis=2)]
    transpose x2 -> x1, local copies, waits for them, and re-layouts: 3.31 us -> 0.1 us  [on_device(): row_map.reshape(wave_count, level_count, rows_here).transpose(1, 2, 0)]
  transfers between devices with their start and end apart: 4 -> 0, of which waited for: 3 -> 0; matrix products, arithmetic and copies ran while one was open for 4% -> 0% of each run, Pallas kernels for 2% -> 0%
where the time goes in v2:
time: 166 us
  Pallas kernels  148 us (89%)
  local copies, waits for them, and re-layouts  13.7 us (8%)
  other arithmetic  3.61 us (2%)
    pallas_call x1, Pallas kernels, gather(): pl.pallas_call(gather_kernel, out_shape=jax.ShapeDtypeStruct((groups * sl...  33.8 us
    pallas_call x1, Pallas kernels, spread(): pl.pallas_call(spread_kernel, out_shape=jax.ShapeDtypeStruct((groups, slo...  33.3 us
    pallas_call x1, Pallas kernels, scatter_rows(): pl.pallas_call(scatter_rows_kernel, out_shape=jax.ShapeDtypeStruct((waves...  31.2 us
    pallas_call x1, Pallas kernels, collect_rows(): pl.pallas_call(collect_rows_kernel, out_shape=jax.ShapeDtypeStruct((group...  27.2 us
    pallas_call x1, Pallas kernels, row_trips(): pl.pallas_call(row_kernel, grid=(rows,), out_shape=(jax.ShapeDtypeStruct(...  16.4 us
    unnamed x15, local copies, waits for them, and re-layouts  6.33 us
    pallas_call x1, Pallas kernels, make_tables(): pl.pallas_call(table_kernel, grid=(rows,), out_shape=jax.ShapeDtypeStruct...  5.72 us

profile of v2, /device:TPU:1, one launch (start us, length us, event | category | flops | bytes accessed | tf_op | source)
XLA Modules:
  0.0 165.7 jit_solution(16080265384767233855)
XLA Ops:
  0.7 0.9 dynamic_slice.6.waves_ref
  1.6 0.8 compare_select_fusion
  2.3 0.6 gather_fusion
  3.0 1.3 gather_fusion.1
  4.3 1.3 convert_divide_fusion.scale_ref
  5.6 0.8 broadcast_select_fusion.points_ref
  6.3 0.7 copy.27.thick_ref
  7.1 0.1 reduce
  7.2 0.7 subtract_bitcast_fusion
  7.9 0.7 copy.28.press_ref
  8.6 0.9 reshape.57
  9.6 0.7 broadcast_in_dim_reshape.3.waves_ref
  10.4 0.9 reshape.55
  11.5 0.2 broadcast_in_dim.21.waves_ref
  11.7 33.3 %spread.1.x_ref = bf16[4,5,144,128]{3,2,1,0:T(8,128)(2,1)S(1)} custom-call(s32[5]{0:T(128)S(1)} %dynamic_slice.6.waves_ref, s32[1,512]{1,0:T(1,128)S(1)} %reshape.56.rows_ref, bf16[20,18,2,1280]{3,2,1,0:T(2,128)(2,1)S(1)} %bitcast.13, bf16[5,1280,512]{2,1,0:T(8,128)(2,1)} %legendre_ref.3), custom_call_target="tpu_custom_call" | custom-call | flops 1321205760 | bytes 6553600 | tf_op jit(solution)/shard_map/spread/pallas_call | solution.py:198
  45.0 31.2 %scatter_rows.1.come_ref = bf16[64,48,128]{2,1,0:T(8,128)(2,1)S(1)} custom-call(bf16[4,5,144,128]{3,2,1,0:T(8,128)(2,1)S(1)} %spread.1.x_ref), custom_call_target="tpu_custom_call" | custom-call | tf_op jit(solution)/shard_map/scatter_rows/pallas_call | solution.py:406
  76.3 0.9 copy-done.3
  77.2 5.7 %tables.1.table_ref = bf16[2,2,1280,768]{3,2,1,0:T(8,128)(2,1)S(1)} custom-call(s32[2]{0:T(128)S(1)} %broadcast_select_fusion.points_ref, f32[1280,128]{1,0:T(8,128)S(1)} %broadcast_in_dim.21.waves_ref), custom_call_target="tpu_custom_call" | custom-call | flops 78643200 | bytes 7864320 | tf_op jit(solution)/shard_map/tables/pallas_call | solution.py:68
  82.9 3.1 %copy-done.1 = bf16[2,2,1280,768]{3,2,1,0:T(8,128)(2,1)} copy-done((bf16[2,2,1280,768]{3,2,1,0:T(8,128)(2,1)}, bf16[2,2,1280,768]{3,2,1,0:T(8,128)(2,1)S(1)}, u32[]{:S(2)}) %copy-start.1) | copy-done | bytes 7864344
  86.0 16.4 %rows.1 = (bf16[64,48,128]{2,1,0:T(8,128)(2,1)}, bf16[2,24,5376]{2,1,0:T(8,128)(2,1)}) custom-call(s32[2]{0:T(128)} %copy-done.5, f32[2]{0:T(128)} %convert_divide_fusion.scale_ref, s32[1,1280]{1,0:T(1,128)} %broadcast_in_dim_reshape.3.waves_ref, f32[24,1]{1,0:T(8,128)} %copy-done.6, f32[24,1]{1,0:T(8,128)} %copy.28.press_ref, ...), custom_call_target="tpu_custom_call" | custom-call | flops 7927234560 | bytes 7864320 | tf_op jit(solution)/shard_map/rows/pallas_call | solution.py:608
  102.4 1.1 copy-done.4
  103.5 27.2 %collect_rows.1.x_ref = bf16[4,5,144,128]{3,2,1,0:T(8,128)(2,1)S(1)} custom-call(bf16[64,48,128]{2,1,0:T(8,128)(2,1)S(1)} %copy-done.4), custom_call_target="tpu_custom_call" | custom-call | tf_op jit(solution)/shard_map/collect_rows/pallas_call | solution.py:453
  130.7 33.8 %gather.15 = bf16[20,18,2,1280]{3,2,1,0:T(2,128)(2,1)S(1)} custom-call(s32[5]{0:T(128)S(1)} %dynamic_slice.6.waves_ref, s32[1,512]{1,0:T(1,128)S(1)} %reshape.56.rows_ref, bf16[4,5,144,128]{3,2,1,0:T(8,128)(2,1)S(1)} %collect_rows.1.x_ref, bf16[5,1280,512]{2,1,0:T(8,128)(2,1)} %legendre_ref.3), custom_call_target="tpu_custom_call" | custom-call | flops 1321205760 | bytes 6553600 | tf_op jit(solution)/shard_map/gather/pallas_call | solution.py:304
  164.5 1.2 copy.30
  (18 shorter events, 0.4 us)
Async XLA Ops:
  0.6 1.7 %copy-start = (s32[512]{0:T(512)S(1)}, s32[512]{0:T(512)}, u32[]{:S(2)}) copy-start(s32[512]{0:T(512)} %param.12) | copy-start | bytes 6148
  0.6 11.1 %copy-start.2 = (bf16[20,3,2,6,1280]{4,2,3,1,0:T(2,128)(2,1)S(1)}, bf16[20,3,2,6,1280]{4,2,3,1,0:T(2,128)(2,1)}, u32[]{:S(2)}) copy-start(bf16[20,3,2,6,1280]{4,2,3,1,0:T(2,128)(2,1)} %param.8) | copy-start | bytes 5529604
  6.3 70.0 %copy-start.5 = (s32[2]{0:T(128)}, s32[2]{0:T(128)S(1)}, u32[]{:S(2)}) copy-start(s32[2]{0:T(128)S(1)} %broadcast_select_fusion.points_ref) | copy-start | bytes 28
  7.1 38.0 %copy-start.6 = (f32[24,1]{1,0:T(8,128)}, f32[24,1]{1,0:T(8,128)S(1)}, u32[]{:S(2)}) copy-start(f32[24,1]{1,0:T(8,128)S(1)} %copy.27.thick_ref) | copy-start | bytes 292
  76.3 0.9 copy-start.3
  82.9 3.1 %copy-start.1 = (bf16[2,2,1280,768]{3,2,1,0:T(8,128)(2,1)}, bf16[2,2,1280,768]{3,2,1,0:T(8,128)(2,1)S(1)}, u32[]{:S(2)}) copy-start(bf16[2,2,1280,768]{3,2,1,0:T(8,128)(2,1)S(1)} %tables.1.table_ref) | copy-start | bytes 23592964
  102.4 1.1 copy-start.4

commit v3 on v1

v3 whole, which is shorter than its diff:
```python
import jax
import jax.numpy as jnp
import numpy as np
from jax import lax
from jax.experimental import pallas as pl
from jax.experimental.pallas import tpu as pltpu
from jax.sharding import PartitionSpec as P

PBUF = 5376
BLOCK = 768
LANES = 128
MESH = pl.DeviceIdType.MESH
NT = (((1,), (1,)), ((), ()))
TN = (((0,), (0,)), ((), ()))
MIB = 1024 * 1024

adiabatic_exponent = 2.0 / 7.0

cos_terms = (0.9999999857, -19.73920338, 64.9390589, -85.44903786, 60.15837722, -25.93212729, 6.478082977)
sin_terms = (6.283185301, -41.34169993, 81.60510632, -76.70254382, 42.02196627, -14.88466424, 3.21649078)


def turn_cos_sin(turns):
    square = turns * turns
    cosine = jnp.full_like(turns, cos_terms[-1])
    for term in cos_terms[-2::-1]:
        cosine = cosine * square + term
    sine = jnp.full_like(turns, sin_terms[-1])
    for term in sin_terms[-2::-1]:
        sine = sine * square + term
    return cosine, sine * turns


def turns_of(product, count, inverse):
    return (product - count * jnp.round(product * inverse)) * inverse


def lev_peer(step):
    level = lax.axis_index("lev")
    return lax.axis_index("wave"), lax.rem(level + step, lax.axis_size("lev"))


def wave_peer(step):
    wave = lax.axis_index("wave")
    core, z, x = lax.rem(wave, 2), lax.rem(lax.div(wave, 2), 8), lax.div(wave, 16)
    z = lax.rem(z + lax.rem(step, 8), 8)
    x = lax.rem(x + lax.rem(lax.div(step, 8), 4), 4)
    core = lax.rem(core + lax.div(step, 32), 2)
    return (x * 8 + z) * 2 + core, lax.axis_index("lev")


def meet(group_count, peer_of, barrier):
    def tell(step, carry):
        pl.semaphore_signal(barrier, inc=1, device_id=peer_of(step), device_id_type=MESH)
        return carry

    lax.fori_loop(1, group_count, tell, 0)


def reorder(values, source):
    count = values.shape[1]
    line = lax.broadcasted_iota(jnp.int32, (16, count), 0)
    digits = jnp.where(line == 0, values // 32, jnp.where(line == 1, values % 32, 0))
    digits = digits.astype(jnp.float32).astype(jnp.bfloat16)
    parts = []
    for at in range(0, count, 256):
        place = lax.broadcasted_iota(jnp.int32, (count, 256), 0)
        choose = jnp.where(place == source[:, at : at + 256], 1.0, 0.0).astype(jnp.bfloat16)
        moved = jnp.dot(digits, choose, preferred_element_type=jnp.float32)
        parts.append(moved[0:1] * 32.0 + moved[1:2])
    return jnp.concatenate(parts, axis=1)


def row_choice(rows, source):
    count = rows.shape[1]
    place = lax.broadcasted_iota(jnp.int32, (count, count), 0).astype(jnp.float32)
    return jnp.where(place == reorder(rows, source), 1.0, 0.0).astype(jnp.bfloat16)


def fill_tables(trig, columns, points, first, last):
    chunk = 64
    lane = lax.broadcasted_iota(jnp.int32, (chunk, LANES), 1).astype(jnp.float32)
    counts = [jnp.full((chunk, LANES), count.astype(jnp.float32), jnp.float32) for count in points]

    def one_chunk(index, carry):
        at = pl.multiple_of(index * chunk, chunk)
        waves = columns[pl.ds(at, chunk), :]
        for row, count in enumerate(counts):
            inverse = 1.0 / count
            cosine, sine = turn_cos_sin(turns_of(waves * lane, count, inverse))
            step_cos, step_sin = turn_cos_sin(turns_of(waves * float(LANES), count, inverse))
            for piece in range(BLOCK // LANES):
                where = pl.ds(piece * LANES, LANES)
                trig[row, 0, pl.ds(at, chunk), where] = cosine.astype(jnp.bfloat16)
                trig[row, 1, pl.ds(at, chunk), where] = (-sine).astype(jnp.bfloat16)
                if piece + 1 < BLOCK // LANES:
                    cosine, sine = (
                        cosine * step_cos - sine * step_sin,
                        sine * step_cos + cosine * step_sin,
                    )
        return carry

    lax.fori_loop(first // chunk, last // chunk, one_chunk, 0)


def unit(size):
    rows = lax.broadcasted_iota(jnp.int32, (size, size), 0)
    return jnp.where(rows == lax.broadcasted_iota(jnp.int32, (size, size), 1), 1.0, 0.0).astype(jnp.bfloat16)


def send_waves(src, dst, send_sem, recv_sem):
    me = lax.axis_index("wave")

    def send(step, carry):
        peer = wave_peer(step)
        pltpu.make_async_remote_copy(
            src_ref=src.at[peer[0]],
            dst_ref=dst.at[me],
            send_sem=send_sem,
            recv_sem=recv_sem,
            device_id=peer,
            device_id_type=MESH,
        ).start()
        return carry

    lax.fori_loop(1, src.shape[0], send, 0)


def wait_waves(ref, sem):
    part = ref.at[pl.ds(0, ref.shape[0] - 1)]
    pltpu.make_async_copy(part, part, sem).wait()


def forward_kernel(
    waves_s, rows_s, points_s, waves_ref, rows_ref, wave_source_ref, row_source_ref, spec_ref, legendre_ref,
    come_ref, order_ref, tables_ref,
    recv, legend, choice, stage, arrived, flat, wide, send, columns, trig,
    own_sem, legend_sem, table_sem, send1, recv1, send2, recv2, send3, recv3, own3,
):
    slots, groups = recv.shape[0], recv.shape[1]
    waves_all = recv.shape[-1]
    senders, lines = come_ref.shape[1], come_ref.shape[2] * come_ref.shape[3]
    wave, level = lax.axis_index("wave"), lax.axis_index("lev")
    device = wave * groups + level
    rows_here = LANES // senders
    tiles = lines // rows_here
    loads = [
        pltpu.make_async_copy(legendre_ref.at[s], legend.at[s], legend_sem.at[s]) for s in range(slots)
    ]
    own = [
        pltpu.make_async_copy(spec_ref.at[level * slots + s], recv.at[s, level], own_sem.at[s])
        for s in range(slots)
    ]
    barrier = pltpu.get_barrier_semaphore()
    meet(groups, lev_peer, barrier)
    meet(senders, wave_peer, barrier)
    for s in range(slots):
        own[s].start()
        loads[s].start()
    pl.semaphore_wait(barrier, groups + senders - 2)

    first, second, own_wave = {}, {}, {}

    def send_coefs(s):
        for step in range(1, groups):
            peer = lax.rem(level + step, groups)
            first[s, step] = pltpu.make_async_remote_copy(
                src_ref=spec_ref.at[peer * slots + s],
                dst_ref=recv.at[s, level],
                send_sem=send1.at[s, step - 1],
                recv_sem=recv1.at[s, step - 1],
                device_id=(wave, peer),
                device_id_type=MESH,
            )
            first[s, step].start()

    send_coefs(0)
    send_coefs(1)
    choice[...] = row_choice(rows_ref[...], row_source_ref[...])
    order_ref[...] = reorder(waves_ref[...], wave_source_ref[...])
    square = lax.broadcasted_iota(jnp.int32, (LANES, LANES), 0) == lax.broadcasted_iota(
        jnp.int32, (LANES, LANES), 1
    )
    for at in range(0, waves_all, LANES):
        diagonal = jnp.where(square, order_ref[:, at : at + LANES], 0.0)
        columns[at : at + LANES, :] = jnp.broadcast_to(
            jnp.sum(diagonal, axis=1, keepdims=True), (LANES, LANES)
        )
    flat[pl.ds(groups * stage.shape[2], flat.shape[0] - groups * stage.shape[2]), :] = jnp.zeros(
        (flat.shape[0] - groups * stage.shape[2], LANES), jnp.bfloat16
    )
    points = [points_s[rows_s[device * rows_here + i]] for i in range(rows_here)]
    identity = unit(LANES)

    def send_rows(s):
        for step in range(1, groups):
            second[s, step].wait_recv()
        flat[: groups * stage.shape[2], :] = arrived[s].reshape(-1, LANES)
        turned = lax.dot_general(identity, flat[...], NT, preferred_element_type=jnp.float32)
        for i in range(rows_here):
            for tile in range(tiles):
                wide[pl.ds(i * tiles + tile, senders, stride=lines), :] = turned[
                    i * senders : (i + 1) * senders, tile * LANES : (tile + 1) * LANES
                ]
        send[s] = wide[...].astype(jnp.bfloat16).reshape(send.shape[1:])
        own_wave[s] = pltpu.make_async_copy(send.at[s, wave], come_ref.at[s, wave], own3.at[s])
        own_wave[s].start()
        send_waves(send.at[s], come_ref.at[s], send3.at[s], recv3.at[s])

    position = lax.broadcasted_iota(jnp.int32, (1, waves_all), 1)
    share = waves_all // slots
    for s in range(slots):
        fill_tables(trig, columns, points, s * share, (s + 1) * share)
        own[s].wait()
        for step in range(1, groups):
            first[s, step].wait_recv()
        loads[s].wait()
        coefs = recv[s].reshape(-1, waves_all)
        keep = jnp.where(position < waves_all - waves_s[device * slots + s], 1.0, 0.0)
        coefs = coefs * jnp.broadcast_to(keep, coefs.shape).astype(jnp.bfloat16)
        fourier = jnp.dot(coefs, legend[s], preferred_element_type=jnp.float32).astype(jnp.bfloat16)
        placed = jnp.dot(fourier, choice[...], preferred_element_type=jnp.float32).astype(jnp.bfloat16)
        for group in range(groups):
            stage[s, group] = placed[:, group * LANES : (group + 1) * LANES]
        for step in range(1, groups):
            peer = lax.rem(level + step, groups)
            second[s, step] = pltpu.make_async_remote_copy(
                src_ref=stage.at[s, peer],
                dst_ref=arrived.at[s, level],
                send_sem=send2.at[s, step - 1],
                recv_sem=recv2.at[s, step - 1],
                device_id=(wave, peer),
                device_id_type=MESH,
            )
            second[s, step].start()
        if s + 2 < slots:
            send_coefs(s + 2)
        arrived[s, level] = stage[s, level]
        if s >= 1:
            send_rows(s - 1)
    store = pltpu.make_async_copy(trig, tables_ref, table_sem)
    store.start()
    send_rows(slots - 1)
    for copy in list(first.values()) + list(second.values()):
        copy.wait_send()
    for s in range(slots):
        own_wave[s].wait()
        wait_waves(send.at[s], send3.at[s])
        wait_waves(come_ref.at[s], recv3.at[s])
    store.wait()


def wave_source(senders, groups, slots):
    places = np.arange(senders * groups * slots).reshape(senders, groups, slots)
    return places.transpose(1, 2, 0).reshape(1, -1).astype(np.int32)


def row_source(senders, groups, rows_here):
    places = np.arange(senders * groups * rows_here).reshape(senders, groups, rows_here)
    return places.transpose(1, 2, 0).reshape(1, -1).astype(np.int32)


def forward(pairs, legendre, wave_map, row_map, points, senders):
    slots, waves_all, rows_all = legendre.shape
    groups = pairs.shape[0] // slots
    columns = groups * pairs.shape[1] * 2
    rows_here = rows_all // (senders * groups)
    tiles = pl.cdiv(groups * columns, LANES)
    lines = rows_here * tiles
    come = (slots, senders, lines // 2, 2, LANES)
    tables = (rows_here, 2, waves_all, BLOCK)
    dma = pltpu.SemaphoreType.DMA
    smem = pl.BlockSpec(memory_space=pltpu.SMEM)
    vmem = pl.BlockSpec(memory_space=pltpu.VMEM)
    anywhere = pl.BlockSpec(memory_space=pl.ANY)
    return pl.pallas_call(
        forward_kernel,
        out_shape=(
            jax.ShapeDtypeStruct(come, jnp.bfloat16),
            jax.ShapeDtypeStruct((1, waves_all), jnp.float32),
            jax.ShapeDtypeStruct(tables, jnp.bfloat16),
        ),
        in_specs=[smem, smem, smem, vmem, vmem, vmem, vmem, anywhere, anywhere],
        out_specs=(vmem, vmem, anywhere),
        scratch_shapes=[
            pltpu.VMEM((slots, groups) + pairs.shape[1:], jnp.bfloat16),
            pltpu.VMEM(legendre.shape, jnp.bfloat16),
            pltpu.VMEM((rows_all, rows_all), jnp.bfloat16),
            pltpu.VMEM((slots, groups, columns, LANES), jnp.bfloat16),
            pltpu.VMEM((slots, groups, columns, LANES), jnp.bfloat16),
            pltpu.VMEM((tiles * LANES, LANES), jnp.bfloat16),
            pltpu.VMEM((senders * lines, LANES), jnp.float32),
            pltpu.VMEM(come, jnp.bfloat16),
            pltpu.VMEM((waves_all, LANES), jnp.float32),
            pltpu.VMEM(tables, jnp.bfloat16),
            dma((slots,)),
            dma((slots,)),
            dma,
            dma((slots, groups - 1)),
            dma((slots, groups - 1)),
            dma((slots, groups - 1)),
            dma((slots, groups - 1)),
            dma((slots,)),
            dma((slots,)),
            dma((slots,)),
        ],
        compiler_params=pltpu.CompilerParams(
            collective_id=1, has_side_effects=True, vmem_limit_bytes=56 * MIB
        ),
        name="forward",
    )(
        wave_map, row_map, points, wave_map[None, :], row_map[None, :],
        jnp.asarray(wave_source(senders, groups, slots)), jnp.asarray(row_source(senders, groups, rows_here)),
        pairs, legendre,
    )


def backward_kernel(
    waves_s, rows_ref, row_source_ref, go_ref, legendre_ref, out_ref,
    back, legend, choice, wide, turned, arrived, stage,
    own_sem, legend_sem, send1, recv1, send2, recv2, send3, recv3, own3,
):
    slots, groups, columns, _ = turned.shape
    senders, lines = go_ref.shape[1], go_ref.shape[2] * go_ref.shape[3]
    waves_all = legend.shape[1]
    wave, level = lax.axis_index("wave"), lax.axis_index("lev")
    device = wave * groups + level
    rows_here = LANES // senders
    tiles = lines // rows_here
    loads = [
        pltpu.make_async_copy(legendre_ref.at[s], legend.at[s], legend_sem.at[s]) for s in range(slots)
    ]
    own_wave = [
        pltpu.make_async_copy(go_ref.at[s, wave], back.at[s, wave], own3.at[s]) for s in range(slots)
    ]
    barrier = pltpu.get_barrier_semaphore()
    meet(groups, lev_peer, barrier)
    meet(senders, wave_peer, barrier)
    for s in range(slots):
        own_wave[s].start()
        loads[s].start()
    pl.semaphore_wait(barrier, groups + senders - 2)

    first, second, own = {}, {}, {}

    def send_rows(s):
        send_waves(go_ref.at[s], back.at[s], send3.at[s], recv3.at[s])

    send_rows(0)
    send_rows(1)
    choice[...] = row_choice(rows_ref[...], row_source_ref[...])
    identity = unit(LANES)
    position = lax.broadcasted_iota(jnp.int32, (1, waves_all), 1)

    def turn(s):
        own_wave[s].wait()
        wait_waves(back.at[s], recv3.at[s])
        wide[...] = back[s].reshape(senders * lines, LANES).astype(jnp.float32)
        placed = jnp.concatenate(
            [
                jnp.concatenate(
                    [wide[pl.ds(i * tiles + tile, senders, stride=lines), :] for tile in range(tiles)], axis=1
                )
                for i in range(rows_here)
            ],
            axis=0,
        ).astype(jnp.bfloat16)
        moved = lax.dot_general(placed, identity, TN, preferred_element_type=jnp.float32)
        turned[s] = moved[: groups * columns].astype(jnp.bfloat16).reshape(groups, columns, LANES)
        for step in range(1, groups):
            peer = lax.rem(level + step, groups)
            first[s, step] = pltpu.make_async_remote_copy(
                src_ref=turned.at[s, peer],
                dst_ref=arrived.at[s, level],
                send_sem=send1.at[s, step - 1],
                recv_sem=recv1.at[s, step - 1],
                device_id=(wave, peer),
                device_id_type=MESH,
            )
            first[s, step].start()
        arrived[s, level] = turned[s, level]

    def finish(s):
        for step in range(1, groups):
            first[s, step].wait_recv()
        loads[s].wait()
        placed = jnp.concatenate([arrived[s, group] for group in range(groups)], axis=1)
        fourier = lax.dot_general(placed, choice[...], NT, preferred_element_type=jnp.float32)
        sums = lax.dot_general(
            fourier.astype(jnp.bfloat16), legend[s], NT, preferred_element_type=jnp.float32
        )
        kept = position < waves_all - waves_s[device * slots + s]
        stage[s] = jnp.where(kept, sums, 0.0).astype(jnp.bfloat16).reshape(stage.shape[1:])
        for step in range(1, groups):
            peer = lax.rem(level + step, groups)
            second[s, step] = pltpu.make_async_remote_copy(
                src_ref=stage.at[s, peer],
                dst_ref=out_ref.at[level * slots + s],
                send_sem=send2.at[s, step - 1],
                recv_sem=recv2.at[s, step - 1],
                device_id=(wave, peer),
                device_id_type=MESH,
            )
            second[s, step].start()
        own[s] = pltpu.make_async_copy(stage.at[s, level], out_ref.at[level * slots + s], own_sem.at[s])
        own[s].start()

    for s in range(slots):
        turn(s)
        if s + 2 < slots:
            send_rows(s + 2)
        if s >= 1:
            finish(s - 1)
    finish(slots - 1)
    for s in range(slots):
        wait_waves(go_ref.at[s], send3.at[s])
        own[s].wait()
    for copy in list(first.values()) + list(second.values()):
        copy.wait_send()
    for copy in second.values():
        copy.wait_recv()


def backward(go, legendre, wave_map, row_map, groups, columns):
    slots, waves_all, rows_all = legendre.shape
    senders, lines = go.shape[1], go.shape[2] * 2
    rows_here = rows_all // (senders * groups)
    pairs = columns // groups // 2
    dma = pltpu.SemaphoreType.DMA
    smem = pl.BlockSpec(memory_space=pltpu.SMEM)
    vmem = pl.BlockSpec(memory_space=pltpu.VMEM)
    anywhere = pl.BlockSpec(memory_space=pl.ANY)
    return pl.pallas_call(
        backward_kernel,
        out_shape=jax.ShapeDtypeStruct((groups * slots, pairs, 2, waves_all), jnp.bfloat16),
        in_specs=[smem, vmem, vmem, vmem, anywhere],
        out_specs=anywhere,
        scratch_shapes=[
            pltpu.VMEM(go.shape, jnp.bfloat16),
            pltpu.VMEM(legendre.shape, jnp.bfloat16),
            pltpu.VMEM((rows_all, rows_all), jnp.bfloat16),
            pltpu.VMEM((senders * lines, LANES), jnp.float32),
            pltpu.VMEM((slots, groups, columns, LANES), jnp.bfloat16),
            pltpu.VMEM((slots, groups, columns, LANES), jnp.bfloat16),
            pltpu.VMEM((slots, groups, pairs, 2, waves_all), jnp.bfloat16),
            dma((slots,)),
            dma((slots,)),
            dma((slots, groups - 1)),
            dma((slots, groups - 1)),
            dma((slots, groups - 1)),
            dma((slots, groups - 1)),
            dma((slots,)),
            dma((slots,)),
            dma((slots,)),
        ],
        compiler_params=pltpu.CompilerParams(
            collective_id=2, has_side_effects=True, vmem_limit_bytes=56 * MIB
        ),
        name="backward",
    )(wave_map, row_map[None, :], jnp.asarray(row_source(senders, groups, rows_here)), go, legendre)


def running_sum(values):
    place = lax.broadcasted_iota(jnp.int32, (8, values.shape[1]), 0)
    before = jnp.zeros((1, values.shape[1]), jnp.float32)
    groups = []
    for start in range(0, values.shape[0], 8):
        part = values[start : start + 8]
        for shift in (1, 2, 4):
            part = part + jnp.where(place >= shift, pltpu.roll(part, shift, 0), 0.0)
        part = part + before
        before = part[7:8]
        groups.append(part)
    return jnp.concatenate(groups, axis=0)


def row_kernel(
    rows_s, points_s, weight_s, waves_ref, thick_ref, order_ref, come_ref, table_ref,
    go_ref, temp_ref, wide, leave, backs, rotated, grid_part, tend,
):
    row = pl.program_id(0)
    slots, senders = come_ref.shape[0], come_ref.shape[1]
    lines = come_ref.shape[2] * come_ref.shape[3]
    waves = waves_ref[...]
    waves_all = waves.shape[1]
    groups = waves_all // (slots * senders)
    span = slots * senders
    levels = thick_ref.shape[1]
    fields, columns = 3 * levels, 6 * levels
    tiles = order_ref.shape[1] // LANES
    device = lax.axis_index("wave") * lax.axis_size("lev") + lax.axis_index("lev")
    grid_row = rows_s[device * pl.num_programs(0) + row]
    count_int = points_s[grid_row]
    count = count_int.astype(jnp.float32)
    inverse = 1.0 / jnp.full((1, 1), count, jnp.float32)
    scale = weight_s[grid_row] * inverse
    blocks = PBUF // BLOCK

    @pl.when(row == 0)
    def _():
        wide[...] = come_ref[...].reshape(slots * senders * lines, LANES).astype(jnp.float32)

    def line_of(slot, tile):
        return slot * (senders * lines) + row * tiles + tile

    placed = jnp.concatenate(
        [
            jnp.concatenate(
                [wide[pl.ds(line_of(slot, tile), senders, stride=lines), :] for tile in range(tiles)], axis=1
            )
            for slot in range(slots)
        ],
        axis=0,
    ).astype(jnp.bfloat16)
    ordered = lax.dot_general(order_ref[...], placed, NT, preferred_element_type=jnp.float32)
    fourier = jnp.concatenate(
        [ordered[group * columns : (group + 1) * columns] for group in range(groups)], axis=1
    )
    kept = 2.0 * waves < count
    weight = jnp.where(kept, jnp.where(waves == 0.0, 1.0, 2.0), 0.0)
    values = fourier * weight
    real, imag = values[:fields], values[fields:]

    starts = lax.broadcasted_iota(jnp.int32, (8, waves_all), 0).astype(jnp.float32) * float(BLOCK)
    phase_cos, phase_sin = turn_cos_sin(turns_of(waves * starts, count, inverse))
    for at in range(0, waves_all, 256):
        lanes = slice(at, at + 256)
        here_real, here_imag = real[:, lanes], imag[:, lanes]
        parts = [], []
        for block in range(blocks):
            cosine = phase_cos[block : block + 1, lanes]
            sine = phase_sin[block : block + 1, lanes]
            parts[0].append(here_real * cosine - here_imag * sine)
            parts[1].append(here_real * sine + here_imag * cosine)
        rotated[:, lanes] = jnp.concatenate(parts[0], axis=0).astype(jnp.bfloat16)
        rotated[:, at + waves_all : at + waves_all + 256] = jnp.concatenate(parts[1], axis=0).astype(jnp.bfloat16)

    for at in range(0, BLOCK, 256):
        right = table_ref[0, :, :, at : at + 256].reshape(2 * waves_all, 256)
        grid_part[:, at : at + 256] = jnp.dot(rotated[...], right, preferred_element_type=jnp.float32)

    above = lax.broadcasted_iota(jnp.int32, (levels, levels), 0) - lax.broadcasted_iota(
        jnp.int32, (levels, levels), 1
    )
    thick_line = jnp.broadcast_to(thick_ref[...], (levels, levels))
    thick = jnp.sum(jnp.where(above == 0, thick_line, 0.0), axis=1, keepdims=True)
    pressure = jnp.sum(jnp.where(above >= 0, thick_line, 0.0), axis=1, keepdims=True) - 0.5 * thick
    factor = adiabatic_exponent / pressure
    place = lax.broadcasted_iota(jnp.int32, (levels, BLOCK), 1)
    for block in range(blocks):
        inside = place < count_int - block * BLOCK
        vorticity = grid_part[pl.ds(block * fields, levels), :]
        spreading = grid_part[pl.ds(block * fields + levels, levels), :]
        thermal = grid_part[pl.ds(block * fields + 2 * levels, levels), :]
        lifting = -running_sum(thick * spreading)
        first = jnp.where(inside, -vorticity * spreading, 0.0)
        second = jnp.where(inside, 0.5 * (vorticity * vorticity - spreading * spreading), 0.0)
        third = jnp.where(inside, thermal * (factor * lifting - spreading), 0.0)
        tend[pl.ds(block * fields, levels), :] = first
        tend[pl.ds(block * fields + levels, levels), :] = second
        tend[pl.ds(block * fields + 2 * levels, levels), :] = third
        temp_ref[0, :, pl.ds(block * BLOCK, BLOCK)] = third.astype(jnp.bfloat16)

    left = tend[...].astype(jnp.bfloat16)
    for at in range(0, waves_all, 256):
        lanes = slice(at, at + 256)
        even = lax.dot_general(left, table_ref[0, 0, lanes, :], NT, preferred_element_type=jnp.float32)
        odd = lax.dot_general(left, table_ref[0, 1, lanes, :], NT, preferred_element_type=jnp.float32)
        real_sum = jnp.zeros((fields, 256), jnp.float32)
        imag_sum = jnp.zeros((fields, 256), jnp.float32)
        for block in range(blocks):
            cosine = phase_cos[block : block + 1, lanes]
            sine = phase_sin[block : block + 1, lanes]
            rows = slice(block * fields, (block + 1) * fields)
            real_sum += cosine * even[rows] + sine * odd[rows]
            imag_sum += cosine * odd[rows] - sine * even[rows]
        keep = jnp.where(kept[:, lanes], scale, 0.0)
        backs[:fields, lanes] = real_sum * keep
        backs[fields:, lanes] = imag_sum * keep

    stacked = jnp.concatenate(
        [backs[:, group * span : (group + 1) * span] for group in range(groups)], axis=0
    ).astype(jnp.bfloat16)
    leaving = lax.dot_general(stacked, order_ref[...], TN, preferred_element_type=jnp.float32)
    for slot in range(slots):
        for tile in range(tiles):
            leave[pl.ds(line_of(slot, tile), senders, stride=lines), :] = leaving[
                slot * senders : (slot + 1) * senders, tile * LANES : (tile + 1) * LANES
            ]

    @pl.when(row == pl.num_programs(0) - 1)
    def _():
        go_ref[...] = leave[...].astype(jnp.bfloat16).reshape(go_ref.shape)


def column_order(levels, groups):
    columns = 6 * levels
    inner = levels // groups
    sender, part, field, group, level = np.meshgrid(
        *(np.arange(n) for n in (groups, 2, 3, groups, inner)), indexing="ij"
    )
    lane = (sender * columns + ((group * 3 + field) * inner + level) * 2 + part).reshape(-1)
    width = pl.cdiv(groups * columns, LANES) * LANES
    return (lane[:, None] == np.arange(width)[None, :]).astype(jnp.bfloat16)


def row_trips(come, tables, waves, row_map, points, row_weight, thickness, groups):
    rows, _, waves_all, _ = tables.shape
    levels = thickness.shape[0]
    columns = 6 * levels
    order = column_order(levels, groups)
    stacked = PBUF // BLOCK * columns // 2
    whole = lambda i: (0, 0)
    whole_come = lambda i: (0,) * come.ndim
    smem = pl.BlockSpec(memory_space=pltpu.SMEM)
    return pl.pallas_call(
        row_kernel,
        grid=(rows,),
        out_shape=(
            jax.ShapeDtypeStruct(come.shape, jnp.bfloat16),
            jax.ShapeDtypeStruct((rows, levels, PBUF), jnp.bfloat16),
        ),
        in_specs=[
            smem,
            smem,
            smem,
            pl.BlockSpec((1, waves_all), whole),
            pl.BlockSpec((1, levels), whole),
            pl.BlockSpec(order.shape, whole),
            pl.BlockSpec(come.shape, whole_come),
            pl.BlockSpec((1, 2, waves_all, BLOCK), lambda i: (i, 0, 0, 0)),
        ],
        out_specs=(
            pl.BlockSpec(come.shape, whole_come),
            pl.BlockSpec((1, levels, PBUF), lambda i: (i, 0, 0)),
        ),
        scratch_shapes=[
            pltpu.VMEM((come.size // LANES, LANES), jnp.float32),
            pltpu.VMEM((come.size // LANES, LANES), jnp.float32),
            pltpu.VMEM((columns, waves_all), jnp.float32),
            pltpu.VMEM((stacked, 2 * waves_all), jnp.bfloat16),
            pltpu.VMEM((stacked, BLOCK), jnp.float32),
            pltpu.VMEM((stacked, BLOCK), jnp.float32),
        ],
        compiler_params=pltpu.CompilerParams(vmem_limit_bytes=56 * MIB),
        cost_estimate=pl.CostEstimate(
            flops=rows * stacked * waves_all * 2 * BLOCK * 4,
            bytes_accessed=rows * waves_all * BLOCK * 4,
            transcendentals=0,
        ),
        name="rows",
    )(row_map, points, row_weight, waves, thickness[None, :], jnp.asarray(order), come, tables)


def on_device(spectral, legendre, wave_map, row_map, points, row_weight, thickness):
    senders, groups = lax.axis_size("wave"), lax.axis_size("lev")
    slots_group, fields, _, levels_here, waves_all = spectral.shape
    columns = 2 * fields * thickness.shape[0]
    pairs = spectral.transpose(0, 1, 3, 2, 4).reshape(slots_group, fields * levels_here, 2, waves_all)
    come, waves, tables = forward(pairs, legendre, wave_map, row_map, points, senders)
    go, row_temps = row_trips(come, tables, waves, row_map, points, row_weight, thickness, groups)
    pairs = backward(go, legendre, wave_map, row_map, groups, columns)
    spec_tend = pairs.reshape(slots_group, fields, levels_here, 2, waves_all).transpose(0, 1, 3, 2, 4)
    return (spec_tend, row_temps)


def solution(mesh):
    return jax.shard_map(
        on_device,
        mesh=mesh,
        in_specs=(
            P("wave", None, None, "lev", None),
            P(("wave", "lev"), None, None),
            P(),
            P(),
            P(),
            P(),
            P(),
        ),
        out_specs=(P("wave", None, None, "lev", None), P(("wave", "lev"), None, None)),
        check_vma=False,
    )
```

time: 231 us -> 128 us (0.55)
  Pallas kernels: 20.3 us -> 122 us
  waiting for transfers between devices: 72.9 us -> 0 us
  blocking collectives: 47.1 us -> 0 us
  local copies, waits for them, and re-layouts: 42.6 us -> 5.29 us
  starting transfers between devices: 30.6 us -> 0 us
  other arithmetic: 8.88 us -> 0 us
  matrix products: 6.66 us -> 0 us
    pallas_call x1 -> x2, Pallas kernels: 5.74 us -> 104 us  [the longest x1 56.3 us: forward(): pl.pallas_call(forward_kernel, out_shape=(jax.ShapeDtypeStruct(come, jnp....]
    all_to_all x4 -> x0, waiting for transfers between devices: 72.9 us -> none  [the longest x1 31.3 us: on_device(): lax.all_to_all(partial_back, 'wave', split_axis=0, concat_axis=2, tiled=T...]
    all_to_all x2 -> x0, blocking collectives: 47.1 us -> none  [the longest x1 26.3 us: on_device(): lax.all_to_all(spec_local, 'lev', split_axis=3, concat_axis=0, tiled=True)]
    all_to_all x4 -> x0, starting transfers between devices: 30.6 us -> none  [the longest x1 14.2 us: on_device(): lax.all_to_all(outgoing, 'wave', split_axis=2, concat_axis=0, tiled=True)]
    all_to_all x11 -> x0, local copies, waits for them, and re-layouts: 15.1 us -> none  [the longest x3 5.07 us: on_device(): lax.all_to_all(returning, 'lev', split_axis=0, concat_axis=2, tiled=True)]
    dot_general x2 -> x0, matrix products: 6.66 us -> none  [the longest x1 5.3 us: on_device(): jnp.einsum('scr,skr->sck', by_latitude, legendre, preferred_element_type=...]
    gather x4 -> x0, local copies, waits for them, and re-layouts: 6.58 us -> none  [the longest x1 2.74 us: on_device(): outgoing = jnp.take(fourier, row_map, axis=2)]
    unnamed x30 -> x1, local copies, waits for them, and re-layouts: 8.96 us -> 4 us
  transfers between devices with their start and end apart: 4 -> 0, of which waited for: 3 -> 0; matrix products, arithmetic and copies ran while one was open for 4% -> 0% of each run, Pallas kernels for 2% -> 0%
where the time goes in v3:
time: 128 us
  Pallas kernels  122 us (95%)
  local copies, waits for them, and re-layouts  5.29 us (4%)
    pallas_call x1, Pallas kernels, forward(): pl.pallas_call(forward_kernel, out_shape=(jax.ShapeDtypeStruct(come, jnp....  56.3 us
    pallas_call x1, Pallas kernels, backward(): pl.pallas_call(backward_kernel, out_shape=jax.ShapeDtypeStruct((groups *...  47.2 us
    pallas_call x1, Pallas kernels, row_trips(): pl.pallas_call(row_kernel, grid=(rows,), out_shape=(jax.ShapeDtypeStruct(...  18.4 us
    unnamed x1, local copies, waits for them, and re-layouts  4 us

profile of v3, /device:TPU:1, one launch (start us, length us, event | category | flops | bytes accessed | tf_op | source)
XLA Modules:
  0.0 127.9 jit_solution(7140730636363084550)
XLA Ops:
  0.6 1.3 %broadcast_in_dim.11.waves_ref = s32[1,1280]{1,0:T(1,128)} reshape(s32[1280]{0:T(1024)} %waves_s.3) | data formatting | bytes 10240 | tf_op jit(solution)/shard_map/broadcast_in_dim | solution.py:312
  1.9 56.3 %forward.1 = (bf16[5,64,5,2,128]{4,3,2,1,0:T(2,128)(2,1)}, f32[1,1280]{1,0:T(1,128)}, bf16[2,2,1280,768]{3,2,1,0:T(8,128)(2,1)}) custom-call(s32[1280]{0:T(1024)} %waves_s.3, s32[512]{0:T(512)} %rows_s.3, s32[512]{0:T(512)} %points_s.3, s32[1,1280]{1,0:T(1,128)} %broadcast_in_dim.11.waves_ref, s32[1,512]{1,0:T(1,128)} %bitcast.10, ...), custom_call_target="tpu_custom_call" | custom-call | tf_op jit(solution)/shard_map/forward/pallas_call | solution.py:276
  58.2 18.4 %rows.1 = (bf16[5,64,5,2,128]{4,3,2,1,0:T(2,128)(2,1)}, bf16[2,24,5376]{2,1,0:T(8,128)(2,1)}) custom-call(s32[512]{0:T(512)} %rows_s.3, s32[512]{0:T(512)} %points_s.3, f32[512]{0:T(512)} %weight_s.1, f32[1,1280]{1,0:T(1,128)} %get-tuple-element.7.waves_ref, f32[1,24]{1,0:T(1,128)} %bitcast.12, bf16[576,640]{1,0:T(8,128)(2,1)} %constant.8.clone.order_ref, ...), custom_call_target="tpu_custom_call" | custom-call | flops 7927234560 | bytes 7864320 | tf_op jit(solution)/shard_map/rows/pallas_call | solution.py:616
  76.7 47.2 %backward.1 = bf16[20,18,2,1280]{3,2,1,0:T(2,128)(2,1)} custom-call(s32[1280]{0:T(1024)} %waves_s.3, s32[1,512]{1,0:T(1,128)} %bitcast.11, s32[1,512]{1,0:T(1,128)} %constant.7.clone.row_source_ref, bf16[5,64,5,2,128]{4,3,2,1,0:T(2,128)(2,1)} %get-tuple-element.10.go_ref, bf16[5,1280,512]{2,1,0:T(8,128)(2,1)} %legendre_ref.3), custom_call_target="tpu_custom_call" | custom-call | tf_op jit(solution)/shard_map/backward/pallas_call | solution.py:433
  123.9 4.0 %copy.14 = bf16[20,3,2,6,1280]{4,2,3,1,0:T(2,128)(2,1)} copy(bf16[20,3,2,6,1280]{4,2,3,1,0:T(2,128)(2,1)} %bitcast.8) | data formatting | bytes 3686400

commit v4 on v0

v4 whole, which is shorter than its diff:
```python
import jax
import jax.numpy as jnp
import numpy as np
from jax import lax
from jax.experimental import pallas as pl
from jax.experimental.pallas import tpu as pltpu
from jax.sharding import PartitionSpec as P

PBUF = 5376
BLOCK = 768
LANES = 128
MESH = pl.DeviceIdType.MESH
NT = (((1,), (1,)), ((), ()))
TN = (((0,), (0,)), ((), ()))
MIB = 1024 * 1024

adiabatic_exponent = 2.0 / 7.0

cos_terms = (0.9999999857, -19.73920338, 64.9390589, -85.44903786, 60.15837722, -25.93212729, 6.478082977)
sin_terms = (6.283185301, -41.34169993, 81.60510632, -76.70254382, 42.02196627, -14.88466424, 3.21649078)


def turn_cos_sin(turns):
    square = turns * turns
    cosine = jnp.full_like(turns, cos_terms[-1])
    for term in cos_terms[-2::-1]:
        cosine = cosine * square + term
    sine = jnp.full_like(turns, sin_terms[-1])
    for term in sin_terms[-2::-1]:
        sine = sine * square + term
    return cosine, sine * turns


def turns_of(product, count, inverse):
    return (product - count * jnp.round(product * inverse)) * inverse


def lev_peer(step):
    level = lax.axis_index("lev")
    return lax.axis_index("wave"), lax.rem(level + step, lax.axis_size("lev"))


ALONG_X, ALONG_Z, CORES = 4, 8, 2
HUBS = ALONG_X * CORES


def hub_and_z():
    wave = lax.axis_index("wave")
    return lax.div(wave, ALONG_Z * CORES) * CORES + lax.rem(wave, CORES), lax.rem(lax.div(wave, CORES), ALONG_Z)


def device_at(hub, z):
    return (lax.div(hub, CORES) * ALONG_Z + z) * CORES + lax.rem(hub, CORES), lax.axis_index("lev")


def hub_peer(step):
    hub, z = hub_and_z()
    return device_at(lax.rem(hub + step, HUBS), z)


def z_peer(step):
    hub, z = hub_and_z()
    return device_at(hub, lax.rem(z + step, ALONG_Z))


def meet(group_count, peer_of, barrier):
    def tell(step, carry):
        pl.semaphore_signal(barrier, inc=1, device_id=peer_of(step), device_id_type=MESH)
        return carry

    lax.fori_loop(1, group_count, tell, 0)


def reorder(values, source):
    count = values.shape[1]
    line = lax.broadcasted_iota(jnp.int32, (16, count), 0)
    digits = jnp.where(line == 0, values // 32, jnp.where(line == 1, values % 32, 0))
    digits = digits.astype(jnp.float32).astype(jnp.bfloat16)
    parts = []
    for at in range(0, count, 256):
        place = lax.broadcasted_iota(jnp.int32, (count, 256), 0)
        choose = jnp.where(place == source[:, at : at + 256], 1.0, 0.0).astype(jnp.bfloat16)
        moved = jnp.dot(digits, choose, preferred_element_type=jnp.float32)
        parts.append(moved[0:1] * 32.0 + moved[1:2])
    return jnp.concatenate(parts, axis=1)


def row_choice(rows, source):
    count = rows.shape[1]
    place = lax.broadcasted_iota(jnp.int32, (count, count), 0).astype(jnp.float32)
    return jnp.where(place == reorder(rows, source), 1.0, 0.0).astype(jnp.bfloat16)


def fill_tables(trig, columns, points, first, last):
    chunk = 64
    lane = lax.broadcasted_iota(jnp.int32, (chunk, LANES), 1).astype(jnp.float32)
    counts = [jnp.full((chunk, LANES), count.astype(jnp.float32), jnp.float32) for count in points]

    def one_chunk(index, carry):
        at = pl.multiple_of(index * chunk, chunk)
        waves = columns[pl.ds(at, chunk), :]
        for row, count in enumerate(counts):
            inverse = 1.0 / count
            cosine, sine = turn_cos_sin(turns_of(waves * lane, count, inverse))
            step_cos, step_sin = turn_cos_sin(turns_of(waves * float(LANES), count, inverse))
            for piece in range(BLOCK // LANES):
                where = pl.ds(piece * LANES, LANES)
                trig[row, 0, pl.ds(at, chunk), where] = cosine.astype(jnp.bfloat16)
                trig[row, 1, pl.ds(at, chunk), where] = (-sine).astype(jnp.bfloat16)
                if piece + 1 < BLOCK // LANES:
                    cosine, sine = (
                        cosine * step_cos - sine * step_sin,
                        sine * step_cos + cosine * step_sin,
                    )
        return carry

    lax.fori_loop(first // chunk, last // chunk, one_chunk, 0)


def unit(size):
    rows = lax.broadcasted_iota(jnp.int32, (size, size), 0)
    return jnp.where(rows == lax.broadcasted_iota(jnp.int32, (size, size), 1), 1.0, 0.0).astype(jnp.bfloat16)


def wait_blocks(ref, sem):
    part = ref.at[pl.ds(0, ref.shape[0] - 1)]
    pltpu.make_async_copy(part, part, sem).wait()


def running_sum(values):
    place = lax.broadcasted_iota(jnp.int32, (8, values.shape[1]), 0)
    before = jnp.zeros((1, values.shape[1]), jnp.float32)
    groups = []
    for start in range(0, values.shape[0], 8):
        part = values[start : start + 8]
        for shift in (1, 2, 4):
            part = part + jnp.where(place >= shift, pltpu.roll(part, shift, 0), 0.0)
        part = part + before
        before = part[7:8]
        groups.append(part)
    return jnp.concatenate(groups, axis=0)


def trip_kernel(
    waves_s, rows_s, points_s, weight_s,
    waves_ref, rows_ref, wave_source_ref, row_source_ref, thick_ref, order_ref, spec_ref, legendre_ref,
    out_ref, temp_ref,
    recv, legend, choice, stage, arrived, flat, wide, send, come, columns, trig, waves_row, phases, grid_part, tend,
    middle, go, middle_back, back, turned, returned, result, order32, order,
    own_sem, legend_sem, order_sem, send1, recv1, send2, recv2, send3, recv3, own3,
    send4, recv4, own4, send5, recv5, send6, recv6, own6,
    send7, recv7, own7, send8, recv8, own8,
):
    slots, groups = recv.shape[0], recv.shape[1]
    waves_all = recv.shape[-1]
    senders, lines = come.shape[1] * come.shape[2], come.shape[3] * come.shape[4]
    hub, z = hub_and_z()
    cells = stage.shape[2]
    used = groups * cells
    wave, level = lax.axis_index("wave"), lax.axis_index("lev")
    device = wave * groups + level
    rows_here = LANES // senders
    tiles = lines // rows_here
    share = groups * senders
    levels = thick_ref.shape[1]
    fields = 3 * levels
    blocks = PBUF // BLOCK
    loads = [
        pltpu.make_async_copy(legendre_ref.at[s], legend.at[s], legend_sem.at[s]) for s in range(slots)
    ]
    own = [
        pltpu.make_async_copy(spec_ref.at[level * slots + s], recv.at[s, level], own_sem.at[s])
        for s in range(slots)
    ]
    barrier = pltpu.get_barrier_semaphore()
    meet(groups, lev_peer, barrier)
    meet(HUBS, hub_peer, barrier)
    meet(ALONG_Z, z_peer, barrier)
    for s in range(slots):
        own[s].start()
        loads[s].start()
    load_order = pltpu.make_async_copy(order_ref, order32, order_sem)
    load_order.start()
    choice[...] = row_choice(rows_ref[...], row_source_ref[...])
    pl.semaphore_wait(barrier, groups + HUBS + ALONG_Z - 3)

    def lev_copies(src_of, dst_of, send_sem, recv_sem, s):
        made = []
        for step in range(1, groups):
            peer = lax.rem(level + step, groups)
            made.append(
                pltpu.make_async_remote_copy(
                    src_ref=src_of(peer),
                    dst_ref=dst_of,
                    send_sem=send_sem.at[s, step - 1],
                    recv_sem=recv_sem.at[s, step - 1],
                    device_id=(wave, peer),
                    device_id_type=MESH,
                )
            )
            made[-1].start()
        return made

    coefs_out, rows_out, rows_back, tend_out = {}, {}, {}, {}
    own_middle, own_come, own_middle_back, own_back, own_out = {}, {}, {}, {}, {}

    def spread(src_of, dst, send_sem, recv_sem, own_sem, peer_of, me, count):
        own_block = pltpu.make_async_copy(src_of(me), dst.at[me], own_sem)
        own_block.start()

        def send_one(step, carry):
            pltpu.make_async_remote_copy(
                src_ref=src_of(lax.rem(me + step, count)),
                dst_ref=dst.at[me],
                send_sem=send_sem,
                recv_sem=recv_sem,
                device_id=peer_of(step),
                device_id_type=MESH,
            ).start()
            return carry

        lax.fori_loop(1, count, send_one, 0)
        return own_block

    def send_coefs(s):
        coefs_out[s] = lev_copies(lambda peer: spec_ref.at[peer * slots + s], recv.at[s, level], send1, recv1, s)

    send_coefs(0)
    send_coefs(1)
    waves_row[...] = reorder(
        jnp.concatenate([waves_ref[line : line + 1, :] for line in range(waves_ref.shape[0])], axis=1),
        wave_source_ref[...],
    )
    square = lax.broadcasted_iota(jnp.int32, (LANES, LANES), 0) == lax.broadcasted_iota(
        jnp.int32, (LANES, LANES), 1
    )
    for at in range(0, waves_all, LANES):
        diagonal = jnp.where(square, waves_row[:, at : at + LANES], 0.0)
        columns[at : at + LANES, :] = jnp.broadcast_to(
            jnp.sum(diagonal, axis=1, keepdims=True), (LANES, LANES)
        )
    load_order.wait()
    order[...] = order32[...].astype(jnp.bfloat16)
    flat[used:, :] = jnp.zeros((flat.shape[0] - used, LANES), jnp.bfloat16)
    identity = unit(LANES)
    position = lax.broadcasted_iota(jnp.int32, (1, waves_all), 1)
    grid_rows = [rows_s[device * rows_here + i] for i in range(rows_here)]
    points = [points_s[row] for row in grid_rows]
    counts = [jnp.full((1, 1), count.astype(jnp.float32), jnp.float32) for count in points]
    scales = [weight_s[row] / count for row, count in zip(grid_rows, counts)]
    starts = lax.broadcasted_iota(jnp.int32, (8, waves_all), 0).astype(jnp.float32) * float(BLOCK)
    for i in range(rows_here):
        phases[i, 0], phases[i, 1] = turn_cos_sin(turns_of(waves_row[...] * starts, counts[i], 1.0 / counts[i]))

    def kept_waves(i, s):
        return 2.0 * waves_row[:, s * share : (s + 1) * share] < counts[i]

    def transform(s):
        own[s].wait()
        for copy in coefs_out[s]:
            copy.wait_recv()
        loads[s].wait()
        coefs = recv[s].reshape(-1, waves_all)
        keep = jnp.where(position < waves_all - waves_s[device * slots + s], 1.0, 0.0)
        coefs = coefs * jnp.broadcast_to(keep, coefs.shape).astype(jnp.bfloat16)
        fourier = jnp.dot(coefs, legend[s], preferred_element_type=jnp.float32).astype(jnp.bfloat16)
        placed = jnp.dot(fourier, choice[...], preferred_element_type=jnp.float32).astype(jnp.bfloat16)
        for group in range(groups):
            stage[s, group] = placed[:, group * LANES : (group + 1) * LANES]
        rows_out[s] = lev_copies(lambda peer: stage.at[s, peer], arrived.at[s, level], send2, recv2, s)
        arrived[s, level] = stage[s, level]

    def send_rows(s):
        for copy in rows_out[s]:
            copy.wait_recv()
        flat[:used, :] = arrived[s].reshape(-1, LANES)
        moved = lax.dot_general(identity, flat[...], NT, preferred_element_type=jnp.float32)
        for i in range(rows_here):
            for tile in range(tiles):
                wide[pl.ds(i * tiles + tile, senders, stride=lines), :] = moved[
                    i * senders : (i + 1) * senders, tile * LANES : (tile + 1) * LANES
                ]
        send[s] = wide[...].astype(jnp.bfloat16).reshape(send.shape[1:])
        own_middle[s] = spread(
            lambda p: send.at[s, p], middle.at[s], send3.at[s], recv3.at[s], own3.at[s], z_peer, z, ALONG_Z
        )

    def hop(s):
        own_middle[s].wait()
        wait_blocks(middle.at[s], recv3.at[s])
        own_come[s] = spread(
            lambda p: middle.at[s, :, p], come.at[s], send7.at[s], recv7.at[s], own7.at[s], hub_peer, hub, HUBS
        )

    def read_lines(ref, s):
        wide[...] = ref[s].reshape(senders * lines, LANES).astype(jnp.float32)
        return jnp.concatenate(
            [
                jnp.concatenate(
                    [wide[pl.ds(i * tiles + tile, senders, stride=lines), :] for tile in range(tiles)], axis=1
                )
                for i in range(rows_here)
            ],
            axis=0,
        ).astype(jnp.bfloat16)

    def absorb(s):
        own_come[s].wait()
        wait_blocks(come.at[s], recv7.at[s])
        ordered = lax.dot_general(order[...], read_lines(come, s), NT, preferred_element_type=jnp.float32)
        lanes = slice(s * share, (s + 1) * share)
        waves = waves_row[:, lanes]
        for i in range(rows_here):
            fourier = jnp.concatenate(
                [
                    ordered[group * cells : (group + 1) * cells, i * senders : (i + 1) * senders]
                    for group in range(groups)
                ],
                axis=1,
            )
            fourier = fourier * jnp.where(kept_waves(i, s), jnp.where(waves == 0.0, 1.0, 2.0), 0.0)
            real, imag = fourier[:fields], fourier[fields:]
            parts = [], []
            for block in range(blocks):
                cosine = phases[i, 0, block : block + 1, lanes]
                sine = phases[i, 1, block : block + 1, lanes]
                parts[0].append(real * cosine - imag * sine)
                parts[1].append(real * sine + imag * cosine)
            left = jnp.concatenate(
                [jnp.concatenate(part, axis=0).astype(jnp.bfloat16) for part in parts], axis=1
            )
            for at in range(0, BLOCK, 256):
                right = trig[i, :, lanes, at : at + 256].reshape(2 * share, 256)
                added = jnp.dot(left, right, preferred_element_type=jnp.float32)
                if s == 0:
                    grid_part[i, :, at : at + 256] = added
                else:
                    grid_part[i, :, at : at + 256] += added

    def products(i):
        above = lax.broadcasted_iota(jnp.int32, (levels, levels), 0) - lax.broadcasted_iota(
            jnp.int32, (levels, levels), 1
        )
        thick_line = jnp.broadcast_to(thick_ref[...], (levels, levels))
        thick = jnp.sum(jnp.where(above == 0, thick_line, 0.0), axis=1, keepdims=True)
        pressure = jnp.sum(jnp.where(above >= 0, thick_line, 0.0), axis=1, keepdims=True) - 0.5 * thick
        factor = adiabatic_exponent / pressure
        place = lax.broadcasted_iota(jnp.int32, (levels, BLOCK), 1)
        parts = []
        for block in range(blocks):
            inside = place < points[i] - block * BLOCK
            at = block * fields
            vorticity = grid_part[i, at : at + levels, :]
            spreading = grid_part[i, at + levels : at + 2 * levels, :]
            thermal = grid_part[i, at + 2 * levels : at + 3 * levels, :]
            lifting = -running_sum(thick * spreading)
            first = jnp.where(inside, -vorticity * spreading, 0.0)
            second = jnp.where(inside, 0.5 * (vorticity * vorticity - spreading * spreading), 0.0)
            third = jnp.where(inside, thermal * (factor * lifting - spreading), 0.0)
            grid_part[i, at : at + levels, :] = first
            grid_part[i, at + levels : at + 2 * levels, :] = second
            grid_part[i, at + 2 * levels : at + 3 * levels, :] = third
            temp_ref[i, :, block * BLOCK : (block + 1) * BLOCK] = third.astype(jnp.bfloat16)
        tend[i] = grid_part[i].astype(jnp.bfloat16)

    def emit(s):
        lanes = slice(s * share, (s + 1) * share)
        pieces = []
        for i in range(rows_here):
            even = lax.dot_general(tend[i], trig[i, 0, lanes, :], NT, preferred_element_type=jnp.float32)
            odd = lax.dot_general(tend[i], trig[i, 1, lanes, :], NT, preferred_element_type=jnp.float32)
            real_sum = jnp.zeros((fields, share), jnp.float32)
            imag_sum = jnp.zeros((fields, share), jnp.float32)
            for block in range(blocks):
                cosine = phases[i, 0, block : block + 1, lanes]
                sine = phases[i, 1, block : block + 1, lanes]
                rows = slice(block * fields, (block + 1) * fields)
                real_sum += cosine * even[rows] + sine * odd[rows]
                imag_sum += cosine * odd[rows] - sine * even[rows]
            sums = jnp.concatenate([real_sum, imag_sum], axis=0) * jnp.where(kept_waves(i, s), scales[i], 0.0)
            pieces.append(
                jnp.concatenate(
                    [sums[:, group * senders : (group + 1) * senders] for group in range(groups)], axis=0
                )
            )
        stacked = jnp.concatenate(pieces, axis=1).astype(jnp.bfloat16)
        leaving = lax.dot_general(stacked, order[...], TN, preferred_element_type=jnp.float32)
        for i in range(rows_here):
            for tile in range(tiles):
                wide[pl.ds(i * tiles + tile, senders, stride=lines), :] = leaving[
                    i * senders : (i + 1) * senders, tile * LANES : (tile + 1) * LANES
                ]
        go[s] = wide[...].astype(jnp.bfloat16).reshape(go.shape[1:])
        own_middle_back[s] = spread(
            lambda p: go.at[s, p], middle_back.at[s], send4.at[s], recv4.at[s], own4.at[s], hub_peer, hub, HUBS
        )

    def hop_back(s):
        own_middle_back[s].wait()
        wait_blocks(middle_back.at[s], recv4.at[s])
        own_back[s] = spread(
            lambda p: middle_back.at[s, :, p], back.at[s], send8.at[s], recv8.at[s], own8.at[s], z_peer, z, ALONG_Z
        )

    def turn(s):
        own_back[s].wait()
        wait_blocks(back.at[s], recv8.at[s])
        moved = lax.dot_general(read_lines(back, s), identity, TN, preferred_element_type=jnp.float32)
        turned[s] = moved[:used].astype(jnp.bfloat16).reshape(groups, cells, LANES)
        rows_back[s] = lev_copies(lambda peer: turned.at[s, peer], returned.at[s, level], send5, recv5, s)
        returned[s, level] = turned[s, level]

    def finish(s):
        for copy in rows_back[s]:
            copy.wait_recv()
        placed = jnp.concatenate([returned[s, group] for group in range(groups)], axis=1)
        fourier = lax.dot_general(placed, choice[...], NT, preferred_element_type=jnp.float32)
        sums = lax.dot_general(
            fourier.astype(jnp.bfloat16), legend[s], NT, preferred_element_type=jnp.float32
        )
        kept = position < waves_all - waves_s[device * slots + s]
        result[s] = jnp.where(kept, sums, 0.0).astype(jnp.bfloat16).reshape(result.shape[1:])
        tend_out[s] = lev_copies(
            lambda peer: result.at[s, peer], out_ref.at[level * slots + s], send6, recv6, s
        )
        own_out[s] = pltpu.make_async_copy(result.at[s, level], out_ref.at[level * slots + s], own6.at[s])
        own_out[s].start()

    for s in range(slots):
        fill_tables(trig, columns, points, s * share, (s + 1) * share)
        transform(s)
        if s + 2 < slots:
            send_coefs(s + 2)
        if s >= 1:
            send_rows(s - 1)
        if s >= 2:
            hop(s - 2)
        if s >= 3:
            absorb(s - 3)
    send_rows(slots - 1)
    hop(slots - 2)
    absorb(slots - 3)
    hop(slots - 1)
    absorb(slots - 2)
    absorb(slots - 1)
    for i in range(rows_here):
        products(i)
    for s in range(slots + 3):
        if s < slots:
            emit(s)
        if 1 <= s <= slots:
            hop_back(s - 1)
        if 2 <= s <= slots + 1:
            turn(s - 2)
        if s >= 3:
            finish(s - 3)
    for s in range(slots):
        for copy in coefs_out[s] + rows_out[s] + rows_back[s] + tend_out[s]:
            copy.wait_send()
        wait_blocks(send.at[s], send3.at[s])
        wait_blocks(come.at[s], send7.at[s])
        wait_blocks(go.at[s], send4.at[s])
        wait_blocks(back.at[s], send8.at[s])
        for copy in tend_out[s]:
            copy.wait_recv()
        own_out[s].wait()


def wave_source(groups, slots):
    places = np.arange(ALONG_X * ALONG_Z * CORES * groups * slots)
    places = places.reshape(ALONG_X, ALONG_Z, CORES, groups, slots).transpose(4, 3, 0, 2, 1)
    return places.reshape(1, -1).astype(np.int32)


def row_source(groups, rows_here):
    places = np.arange(ALONG_X * ALONG_Z * CORES * groups * rows_here)
    places = places.reshape(ALONG_X, ALONG_Z, CORES, groups, rows_here).transpose(3, 4, 1, 0, 2)
    return places.reshape(1, -1).astype(np.int32)


def column_order(levels, groups):
    columns = 6 * levels
    inner = levels // groups
    sender, part, field, group, level = np.meshgrid(
        *(np.arange(n) for n in (groups, 2, 3, groups, inner)), indexing="ij"
    )
    lane = (sender * columns + ((group * 3 + field) * inner + level) * 2 + part).reshape(-1)
    width = pl.cdiv(groups * columns, LANES) * LANES
    return (lane[:, None] == np.arange(width)[None, :]).astype(np.float32)


def round_trip(pairs, legendre, wave_map, row_map, points, row_weight, thickness, senders):
    slots, waves_all, rows_all = legendre.shape
    groups = pairs.shape[0] // slots
    levels = thickness.shape[0]
    columns = 6 * levels
    rows_here = rows_all // (senders * groups)
    tiles = pl.cdiv(groups * columns, LANES)
    lines = rows_here * tiles
    stacked = PBUF // BLOCK * columns // 2
    by_z = (slots, ALONG_Z, HUBS, lines // 2, 2, LANES)
    by_hub = (slots, HUBS, ALONG_Z, lines // 2, 2, LANES)
    order = column_order(levels, groups)
    by_group = (slots, groups, columns, LANES)
    by_level = (slots, groups) + pairs.shape[1:]
    bf16, f32 = jnp.bfloat16, jnp.float32
    dma = pltpu.SemaphoreType.DMA
    lev_sem = dma((slots, groups - 1))
    slot_sem = dma((slots,))
    smem = pl.BlockSpec(memory_space=pltpu.SMEM)
    vmem = pl.BlockSpec(memory_space=pltpu.VMEM)
    anywhere = pl.BlockSpec(memory_space=pl.ANY)
    return pl.pallas_call(
        trip_kernel,
        out_shape=(
            jax.ShapeDtypeStruct(pairs.shape, bf16),
            jax.ShapeDtypeStruct((rows_here, levels, PBUF), bf16),
        ),
        in_specs=[smem] * 4 + [vmem] * 5 + [anywhere] * 3,
        out_specs=(anywhere, vmem),
        scratch_shapes=[
            pltpu.VMEM(by_level, bf16),
            pltpu.VMEM(legendre.shape, bf16),
            pltpu.VMEM((rows_all, rows_all), bf16),
            pltpu.VMEM(by_group, bf16),
            pltpu.VMEM(by_group, bf16),
            pltpu.VMEM((tiles * LANES, LANES), bf16),
            pltpu.VMEM((senders * lines, LANES), f32),
            pltpu.VMEM(by_z, bf16),
            pltpu.VMEM(by_hub, bf16),
            pltpu.VMEM((waves_all, LANES), f32),
            pltpu.VMEM((rows_here, 2, waves_all, BLOCK), bf16),
            pltpu.VMEM((1, waves_all), f32),
            pltpu.VMEM((rows_here, 2, 8, waves_all), f32),
            pltpu.VMEM((rows_here, stacked, BLOCK), f32),
            pltpu.VMEM((rows_here, stacked, BLOCK), bf16),
            pltpu.VMEM(by_z, bf16),
            pltpu.VMEM(by_hub, bf16),
            pltpu.VMEM(by_hub, bf16),
            pltpu.VMEM(by_z, bf16),
            pltpu.VMEM(by_group, bf16),
            pltpu.VMEM(by_group, bf16),
            pltpu.VMEM(by_level, bf16),
            pltpu.VMEM(order.shape, f32),
            pltpu.VMEM(order.shape, bf16),
            slot_sem, slot_sem, dma, lev_sem, lev_sem, lev_sem, lev_sem, slot_sem, slot_sem, slot_sem,
            slot_sem, slot_sem, slot_sem, lev_sem, lev_sem, lev_sem, lev_sem, slot_sem,
            slot_sem, slot_sem, slot_sem, slot_sem, slot_sem, slot_sem,
        ],
        compiler_params=pltpu.CompilerParams(
            collective_id=1, has_side_effects=True, vmem_limit_bytes=56 * MIB
        ),
        name="trip",
    )(
        wave_map, row_map, points, row_weight, wave_map.reshape(-1, LANES), row_map[None, :],
        jnp.asarray(wave_source(groups, slots)), jnp.asarray(row_source(groups, rows_here)),
        thickness[None, :], jnp.asarray(order), pairs, legendre,
    )


def settle_kernel(*refs):
    count = (len(refs) - 2) // 3
    sources, targets, held = refs[:count], refs[count : 2 * count], refs[2 * count : 3 * count]
    in_sems, out_sems = refs[-2:]
    blocks = [(which, block) for which in range(count) for block in range(sources[which].shape[0])]
    arriving, leaving = [], []
    for place, (which, block) in enumerate(blocks):
        arriving.append(
            pltpu.make_async_copy(sources[which].at[block], held[which].at[block], in_sems.at[place])
        )
        arriving[-1].start()
    for place, (which, block) in enumerate(blocks):
        arriving[place].wait()
        leaving.append(
            pltpu.make_async_copy(held[which].at[block], targets[which].at[block], out_sems.at[place])
        )
        leaving[-1].start()
    for copy in leaving:
        copy.wait()


def settle(*arrays):
    anywhere = pl.BlockSpec(memory_space=pl.ANY)
    return pl.pallas_call(
        settle_kernel,
        out_shape=tuple(jax.ShapeDtypeStruct(array.shape, array.dtype) for array in arrays),
        in_specs=[anywhere] * len(arrays),
        out_specs=(anywhere,) * len(arrays),
        scratch_shapes=[pltpu.VMEM(array.shape, array.dtype) for array in arrays]
        + [pltpu.SemaphoreType.DMA((sum(array.shape[0] for array in arrays),))] * 2,
        compiler_params=pltpu.CompilerParams(vmem_limit_bytes=56 * MIB),
        name="settle",
    )(*arrays)


def on_device(spectral, legendre, wave_map, row_map, points, row_weight, thickness):
    slots_group, fields, _, levels_here, waves_all = spectral.shape
    pairs = spectral.transpose(0, 1, 3, 2, 4).reshape(slots_group, fields * levels_here, 2, waves_all)
    pairs, row_temps = round_trip(
        pairs, legendre, wave_map, row_map, points, row_weight, thickness, lax.axis_size("wave")
    )
    pairs, row_temps = settle(pairs, row_temps)
    spec_tend = pairs.reshape(slots_group, fields, levels_here, 2, waves_all).transpose(0, 1, 3, 2, 4)
    return (spec_tend, row_temps)


def solution(mesh):
    return jax.shard_map(
        on_device,
        mesh=mesh,
        in_specs=(
            P("wave", None, None, "lev", None),
            P(("wave", "lev"), None, None),
            P(),
            P(),
            P(),
            P(),
            P(),
        ),
        out_specs=(P("wave", None, None, "lev", None), P(("wave", "lev"), None, None)),
        check_vma=False,
    )
```

time: 1120 us -> 107 us (0.10)
  other arithmetic: 782 us -> 0 us
  Pallas kernels: 0 us -> 106 us
  starting transfers between devices: 93.9 us -> 0 us
  waiting for transfers between devices: 83.6 us -> 0 us
  local copies, waits for them, and re-layouts: 58 us -> 0 us
  matrix products: 54.2 us -> 0 us
  blocking collectives: 39.9 us -> 0 us
    convert_element_type x30 -> x0, other arithmetic: 730 us -> none  [the longest x13 728 us: one_block(): jnp.where(active, block_cos, 0.0).astype(jnp.bfloat16)]
    pallas_call x0 -> x2, Pallas kernels: none -> 106 us  [the longest x1 104 us: round_trip(): pl.pallas_call(trip_kernel, out_shape=(jax.ShapeDtypeStruct(pairs.shape,...]
    all_to_all x4 -> x0, starting transfers between devices: 93.9 us -> none  [the longest x1 70.8 us: on_device(): lax.all_to_all(partial_back, 'wave', split_axis=0, concat_axis=2, tiled=T...]
    all_to_all x4 -> x0, waiting for transfers between devices: 83.6 us -> none  [the longest x1 31.5 us: on_device(): lax.all_to_all(partial_back, 'wave', split_axis=0, concat_axis=2, tiled=T...]
    dot_general x28 -> x0, matrix products: 54.2 us -> none  [the longest x13 38 us: one_block(): lax.dot_general(tendency.reshape(3 * levels, block_width), tables, (((1,)...]
    all_to_all x2 -> x0, blocking collectives: 39.9 us -> none  [the longest x1 26.3 us: on_device(): lax.all_to_all(spec_local, 'lev', split_axis=3, concat_axis=0, tiled=True)]
    all_to_all x10 -> x0, local copies, waits for them, and re-layouts: 13.6 us -> none  [the longest x3 5.07 us: on_device(): lax.all_to_all(returning, 'lev', split_axis=0, concat_axis=2, tiled=True)]
    cos x13 -> x0, other arithmetic: 12 us -> none  [one_block(): phase_cos = jnp.cos(phase)[:, None]]
  transfers between devices with their start and end apart: 4 -> 0, of which waited for: 4 -> 0; matrix products, arithmetic and copies ran while one was open for 1% -> 0% of each run, Pallas kernels for 0% -> 0%
where the time goes in v4:
time: 107 us
  Pallas kernels  106 us (99%)
    pallas_call x1, Pallas kernels, round_trip(): pl.pallas_call(trip_kernel, out_shape=(jax.ShapeDtypeStruct(pairs.shape,...  104 us
    pallas_call x1, Pallas kernels, settle(): pl.pallas_call(settle_kernel, out_shape=tuple((jax.ShapeDtypeStruct(array...  2.78 us

profile of v4, /device:TPU:1, one launch (start us, length us, event | category | flops | bytes accessed | tf_op | source)
XLA Modules:
  0.0 107.3 jit_solution(4656051144141019113)
XLA Ops:
  0.6 103.7 %trip.1 = (bf16[20,18,2,1280]{3,2,1,0:T(2,128)(2,1)}, bf16[2,24,5376]{2,1,0:T(8,128)(2,1)}) custom-call(s32[1280]{0:T(1024)} %waves_s.1, s32[512]{0:T(512)} %rows_s.1, s32[512]{0:T(512)} %points_s.1, f32[512]{0:T(512)} %weight_s.1, s32[10,128]{1,0:T(8,128)} %bitcast.10, s32[1,512]{1,0:T(1,128)} %bitcast.11, s32[1,1280]{1,0:T(1,128)} %constant.6.clone.wave_source_ref, ...), custom_call_target="tpu_custom_call" | custom-call | tf_op jit(solution)/shard_map/trip/pallas_call | solution.py:513
  104.3 2.8 %settle.1 = (bf16[20,18,2,1280]{3,2,1,0:T(2,128)(2,1)}, bf16[2,24,5376]{2,1,0:T(8,128)(2,1)}) custom-call(bf16[20,18,2,1280]{3,2,1,0:T(2,128)(2,1)} %get-tuple-element.6.refs_0_, bf16[2,24,5376]{2,1,0:T(8,128)(2,1)} %get-tuple-element.7.refs_1_), custom_call_target="tpu_custom_call" | custom-call | tf_op jit(solution)/shard_map/settle/pallas_call | solution.py:584

commit v5 on v4

--- a/solution.py
+++ b/solution.py
@@ -144,8 +144,8 @@
 def trip_kernel(
     waves_s, rows_s, points_s, weight_s,
     waves_ref, rows_ref, wave_source_ref, row_source_ref, thick_ref, order_ref, spec_ref, legendre_ref,
-    out_ref, temp_ref,
-    recv, legend, choice, stage, arrived, flat, wide, send, come, columns, trig, waves_row, phases, grid_part, tend,
+    out_ref, temp_out_ref,
+    temp_ref, temp_sem, recv, legend, choice, stage, arrived, flat, wide, send, come, columns, trig, waves_row, phases, grid_part, tend,
     middle, go, middle_back, back, turned, returned, result, order32, order,
     own_sem, legend_sem, order_sem, send1, recv1, send2, recv2, send3, recv3, own3,
     send4, recv4, own4, send5, recv5, send6, recv6, own6,
@@ -445,6 +445,8 @@
     absorb(slots - 1)
     for i in range(rows_here):
         products(i)
+    store = pltpu.make_async_copy(temp_ref, temp_out_ref, temp_sem)
+    store.start()
     for s in range(slots + 3):
         if s < slots:
             emit(s)
@@ -464,6 +466,7 @@
         for copy in tend_out[s]:
             copy.wait_recv()
         own_out[s].wait()
+    store.wait()
 
 
 def wave_source(groups, slots):
@@ -517,8 +520,10 @@
             jax.ShapeDtypeStruct((rows_here, levels, PBUF), bf16),
         ),
         in_specs=[smem] * 4 + [vmem] * 5 + [anywhere] * 3,
-        out_specs=(anywhere, vmem),
+        out_specs=(anywhere, anywhere),
         scratch_shapes=[
+            pltpu.VMEM((rows_here, levels, PBUF), bf16),
+            dma,
             pltpu.VMEM(by_level, bf16),
             pltpu.VMEM(legendre.shape, bf16),
             pltpu.VMEM((rows_all, rows_all), bf16),

time: 107 us -> 107 us (level)
  no operation moved by 1% of the time
where the time goes in v5:
time: 107 us; the launch traced here: 106 us
  Pallas kernels  106 us (99%)
    pallas_call x1, Pallas kernels, round_trip(): pl.pallas_call(trip_kernel, out_shape=(jax.ShapeDtypeStruct(pairs.shape,...  103 us
    pallas_call x1, Pallas kernels, settle(): pl.pallas_call(settle_kernel, out_shape=tuple((jax.ShapeDtypeStruct(array...  2.78 us

profile of v5, /device:TPU:1, one launch (start us, length us, event | category | flops | bytes accessed | tf_op | source)
XLA Modules:
  0.0 106.5 jit_solution(17692708946799225815)
XLA Ops:
  0.6 102.9 %trip.1 = (bf16[20,18,2,1280]{3,2,1,0:T(2,128)(2,1)}, bf16[2,24,5376]{2,1,0:T(8,128)(2,1)}) custom-call(s32[1280]{0:T(1024)} %waves_s.1, s32[512]{0:T(512)} %rows_s.1, s32[512]{0:T(512)} %points_s.1, f32[512]{0:T(512)} %weight_s.1, s32[10,128]{1,0:T(8,128)} %bitcast.10, s32[1,512]{1,0:T(1,128)} %bitcast.11, s32[1,1280]{1,0:T(1,128)} %constant.6.clone.wave_source_ref, ...), custom_call_target="tpu_custom_call" | custom-call | tf_op jit(solution)/shard_map/trip/pallas_call | solution.py:516
  103.5 2.8 %settle.1 = (bf16[20,18,2,1280]{3,2,1,0:T(2,128)(2,1)}, bf16[2,24,5376]{2,1,0:T(8,128)(2,1)}) custom-call(bf16[20,18,2,1280]{3,2,1,0:T(2,128)(2,1)} %get-tuple-element.6.refs_0_, bf16[2,24,5376]{2,1,0:T(8,128)(2,1)} %get-tuple-element.7.refs_1_), custom_call_target="tpu_custom_call" | custom-call | tf_op jit(solution)/shard_map/settle/pallas_call | solution.py:589
